TPU v7x, 128 devices: a whole 4x4x4 slice. The times are simulated.
128 devices in a mesh: lat: 16 (over z, x_hi, core), lon: 8 (over y, x_lo).
Axes of the slice: x: 4 (x_hi: 2, x_lo: 2; x = x_hi * 2 + x_lo), y: 4, z: 4, core: 2. Of those that a mesh axis runs over, the one named last changes fastest.
Arguments:
- winds: float32 [2, 16, 1440, 2880], P(None, None, 'lat', 'lon'), may hold values from -6 to 6
- theta: float32 [16, 1440, 2880], P(None, 'lat', 'lon'), may hold values from -6 to 6
- thick: float32 [16, 1440, 2880], P(None, 'lat', 'lon'), may hold values from 0.5 to 1.5
- polar_rows: int32 [480], replicated, may hold values from 0 to 1439, as said below
- cutoffs: int32 [480], replicated, may hold values from 1 to 719, as said below
Outputs:
- new_winds: float32 [2, 16, 1440, 2880], P(None, None, 'lat', 'lon')
- new_theta: float32 [16, 1440, 2880], P(None, 'lat', 'lon')
- new_thick: float32 [16, 1440, 2880], P(None, 'lat', 'lon')
Inputs may be any that keep to these rules, and one draw needn't show every extreme that they name: `polar_rows`: each row is listed once, in an order drawn from the seed. The listed rows are a run of rows from row 0 up together with a run of rows ending at row 1439; each run has between 180 and 300 rows, so no row of the middle half of the latitudes is listed. `cutoffs`: rows 0 and 1439 have cutoff 1, and the listed row of each run that lies farthest from its pole has cutoff 720 - 1. Any other listed row that lies d rows from its nearest pole (d = 0 at the pole) has a cutoff between min(d + 1, 719) and min(2 (d + 1), 719).
All inputs are finite; a program needn't handle non-finite values.
Results may differ from a plain program's by a relative error of at most 0.000071.
Values sent between devices are 32-bit elements; how exact they have to be, the bound alone decides.
A program may use at most 192 MiB of HBM per device.

v0:
```python
import jax
import jax.numpy as jnp
from jax import lax
from jax.sharding import PartitionSpec as P

HIGH = lax.Precision.HIGHEST


def padded(cells, sides, width, closed):
    for axis, dim in sides:
        count = lax.axis_size(axis)
        ends = count if closed else count - 1
        head = lax.slice_in_dim(cells, 0, width, axis=dim)
        tail = lax.slice_in_dim(cells, cells.shape[dim] - width, cells.shape[dim], axis=dim)
        cells = jnp.concatenate(
            [
                lax.ppermute(tail, axis, [(i, (i + 1) % count) for i in range(ends)]),
                cells,
                lax.ppermute(head, axis, [((i + 1) % count, i) for i in range(ends)]),
            ],
            axis=dim,
        )
    return cells


def row_marks(block, count, polar_rows, cutoffs):
    global_rows = block * count + jnp.arange(count, dtype=jnp.int32)
    hits = polar_rows[None, :] == global_rows[:, None]
    listed = jnp.any(hits, axis=1)
    limit = jnp.sum(jnp.where(hits, cutoffs[None, :], 0), axis=1)
    return (listed, limit)


def truncate_rows(rows, limit):
    length = rows.shape[2]
    waves = length // 4
    points = jnp.arange(length, dtype=jnp.int32)
    wave = jnp.arange(waves, dtype=jnp.int32)
    angle = (points[:, None] * wave[None, :] % length).astype(jnp.float32) * (2.0 * jnp.pi / length)
    forward = jnp.concatenate([jnp.cos(angle), jnp.sin(angle)], axis=1)
    weight = jnp.where(wave == 0, 1.0, 2.0).astype(jnp.float32) / length
    inverse = jnp.concatenate(
        [jnp.cos(angle) * weight[None, :], jnp.sin(angle) * weight[None, :]], axis=1
    ).T
    spec = jnp.einsum("pqn,nk->pqk", rows, forward, precision=HIGH)
    keep = (wave[None, :] <= limit[:, None]).astype(jnp.float32)
    spec = spec * jnp.concatenate([keep, keep], axis=1)[None, :, :]
    return jnp.einsum("pqk,kn->pqn", spec, inverse, precision=HIGH)


def filter_rows(stacked, limit):
    moved = lax.all_to_all(stacked, "lon", split_axis=0, concat_axis=2, tiled=True)
    smooth = truncate_rows(moved, limit)
    return lax.all_to_all(smooth, "lon", split_axis=2, concat_axis=0, tiled=True)


def body(winds, theta, thick, polar_rows, cutoffs):
    levels = theta.shape[0]
    count = theta.shape[1]
    width = theta.shape[2]
    lat_size = lax.axis_size("lat")
    total_rows = count * lat_size
    block = lax.axis_index("lat")
    stacked = jnp.concatenate([winds.reshape(2 * levels, count, width), theta, thick], axis=0)
    listed, limit = row_marks(block, count, polar_rows, cutoffs)
    smooth = filter_rows(stacked, limit)
    state = jnp.where(listed[None, :, None], smooth, stacked)
    lat_pad = padded(state, (("lat", 1),), 1, False)
    lon_pad = padded(state, (("lon", 2),), 1, True)
    padded_rows = block * count - 1 + jnp.arange(count + 2, dtype=jnp.int32)
    cos_pad = jnp.sin((padded_rows.astype(jnp.float32) + 0.5) * (jnp.pi / total_rows))[
        None, :, None
    ]
    centre = (block * count + jnp.arange(count, dtype=jnp.int32)).astype(jnp.float32) + 0.5
    coslat = jnp.sin(centre * (jnp.pi / total_rows))[None, :, None]
    sinlat = (-jnp.cos(centre * (jnp.pi / total_rows)))[None, :, None]

    def diff_lon(field):
        return (field[:, :, 2:] - field[:, :, :-2]) * 0.5

    def diff_lat(field):
        return (field[:, 2:, :] - field[:, :-2, :]) * 0.5

    def part(field, index):
        return field[index * levels : (index + 1) * levels]

    west_u, west_v, west_t, west_h = [part(lon_pad, k) for k in range(4)]
    north_u, north_v, north_t, north_h = [part(lat_pad, k) for k in range(4)]
    wind_u, wind_v, temper, layer = [part(state, k) for k in range(4)]
    new_h = (
        layer
        - 0.05 * diff_lon(west_u * west_h) / coslat
        - 0.2 * diff_lat(north_v * north_h * cos_pad) / coslat
    )
    new_t = temper - 0.05 * wind_u * diff_lon(west_t) / coslat - 0.2 * wind_v * diff_lat(north_t)
    new_u = (
        wind_u
        - 0.05 * wind_u * diff_lon(west_u) / coslat
        - 0.2 * wind_v * diff_lat(north_u)
        - 0.1 * diff_lon(west_h) / coslat
        + 0.3 * sinlat * wind_v
    )
    new_v = (
        wind_v
        - 0.05 * wind_u * diff_lon(west_v) / coslat
        - 0.2 * wind_v * diff_lat(north_v)
        - 0.3 * diff_lat(north_h)
        - 0.3 * sinlat * wind_u
    )
    return (jnp.stack([new_u, new_v]), new_t, new_h)


def solution(mesh):
    in_specs = (P(None, None, "lat", "lon"), P(None, "lat", "lon"), P(None, "lat", "lon"), P(), P())
    out_specs = (P(None, None, "lat", "lon"), P(None, "lat", "lon"), P(None, "lat", "lon"))
    return jax.shard_map(body, mesh=mesh, in_specs=in_specs, out_specs=out_specs, check_vma=False)
```

profile of v0, /device:TPU:97, one launch (start us, length us, event | category | flops | bytes accessed | tf_op | source)
XLA Modules:
  0.0 474.3 jit_solution(16336102567361754950)
XLA Ops:
  0.7 5.2 %copy.31 = f32[2,16,90,360]{3,1,0,2:T(8,128)} copy(f32[2,16,90,360]{3,1,2,0:T(8,128)} %param.5) | data formatting | bytes 8294400 | tf_op args[0]
  8.6 8.8 %copy.32 = f32[64,90,360]{2,1,0:T(8,128)} copy(f32[64,90,360]{2,0,1:T(8,128)S(1)} %pad_maximum_fusion) | data formatting | bytes 16588800 | tf_op jit(solution)/shard_map/concatenate | solution.py:64
  17.4 5.5 %all-to-all-start = ((f32[64,90,360]{2,1,0:T(8,128)}), f32[64,90,360]{2,1,0:T(8,128)}, u32[]{:S(2)}, u32[]{:S(2)}) async-start(f32[64,90,360]{2,1,0:T(8,128)} %copy.32), calls=%async_computation | async-start | bytes 18874368 | tf_op jit(solution)/shard_map/all_to_all | solution.py:52
  23.4 36.6 %fusion.11 = (f32[2880,720]{0,1:T(8,128)}, f32[2880,720]{0,1:T(8,128)}) fusion(), kind=kLoop, calls=%fused_computation.24 | loop fusion | flops 18662400 | bytes 16588800 | tf_op jit(solution)/shard_map/sin | solution.py:40
  60.0 36.9 %broadcast_multiply_fusion.1 = (f32[2880,720]{0,1:T(8,128)}, f32[2880,720]{0,1:T(8,128)}) fusion(f32[720]{0:T(1024)S(1)} %select_multiply_fusion), kind=kLoop, calls=%fused_computation.36 | loop fusion | flops 22809600 | bytes 16591680 | tf_op jit(solution)/shard_map/mul | solution.py:43
  96.9 30.7 %all-to-all-done = f32[64,90,360]{2,1,0:T(8,128)} async-done(((f32[64,90,360]{2,1,0:T(8,128)}), f32[64,90,360]{2,1,0:T(8,128)}, u32[]{:S(2)}, u32[]{:S(2)}) %all-to-all-start) | async-done | bytes 8294432 | tf_op jit(solution)/shard_map/all_to_all | solution.py:52
  127.6 12.3 %copy.50 = f32[8,8,90,360]{3,0,1,2:T(8,128)} copy(f32[8,8,90,360]{3,2,1,0:T(8,128)} %bitcast.1) | data formatting | bytes 16588800 | tf_op jit(solution)/shard_map/all_to_all | solution.py:52
  139.9 10.5 %all_to_all.29 = f32[8,90,2880]{2,0,1:T(8,128)} reshape(f32[8,90,8,360]{3,2,0,1:T(8,128)} %bitcast.29) | data formatting | bytes 16588800 | tf_op jit(solution)/shard_map/all_to_all | solution.py:52
  150.4 53.3 %fusion = f32[8,90,1440]{2,1,0:T(8,128)S(1)} fusion(f32[2880,720]{0,1:T(8,128)} %get-tuple-element.11, f32[2880,720]{0,1:T(8,128)} %get-tuple-element.12, f32[8,90,2880]{2,0,1:T(8,128)} %all_to_all.29), kind=kOutput, calls=%fused_computation.1 | convolution fusion | flops 35835953152 | bytes 29030400 | tf_op jit(solution)/shard_map/pqn,nk->pqk/dot_general | solution.py:45
  203.7 51.3 %fusion.3 = f32[8,90,2880]{2,1,0:T(8,128)} fusion(f32[2880,720]{0,1:T(8,128)} %get-tuple-element.10, f32[2880,720]{0,1:T(8,128)} %get-tuple-element.9, f32[8,90,1440]{2,1,0:T(8,128)S(1)} %fusion, f32[90,1440]{1,0:T(8,128)S(1)} %add_convert_fusion), kind=kOutput, calls=%fused_computation.5 | convolution fusion | flops 35836993536 | bytes 29548800 | tf_op jit(solution)/shard_map/pqk,kn->pqn/dot_general | solution.py:48
  255.0 11.4 %copy.35 = f32[8,90,2880]{1,0,2:T(8,128)} copy(f32[8,90,2880]{2,1,0:T(8,128)} %fusion.3) | data formatting | bytes 16588800 | tf_op jit(solution)/shard_map/pqk,kn->pqn/dot_general | solution.py:48
  266.4 5.3 %all-to-all-start.1 = ((f32[8,90,2880]{1,0,2:T(8,128)}), f32[8,90,2880]{1,0,2:T(8,128)}, u32[]{:S(2)}, u32[]{:S(2)}) async-start(f32[8,90,2880]{1,0,2:T(8,128)} %copy.35), calls=%async_computation.1 | async-start | bytes 23592960 | tf_op jit(solution)/shard_map/all_to_all | solution.py:54
  272.0 128.8 %all-to-all-done.1 = f32[8,90,2880]{1,0,2:T(8,128)} async-done(((f32[8,90,2880]{1,0,2:T(8,128)}), f32[8,90,2880]{1,0,2:T(8,128)}, u32[]{:S(2)}, u32[]{:S(2)}) %all-to-all-start.1) | async-done | bytes 8294432 | tf_op jit(solution)/shard_map/all_to_all | solution.py:54
  400.8 11.6 %copy.37 = f32[8,8,90,360]{3,1,0,2:T(8,128)} copy(f32[8,8,90,360]{2,1,3,0:T(8,128)} %bitcast.7) | data formatting | bytes 16588800 | tf_op jit(solution)/shard_map/all_to_all | solution.py:54
  412.4 6.5 %bitcast_select_fusion = f32[64,90,360]{2,0,1:T(8,128)S(1)} fusion(f32[8,8,90,360]{3,1,0,2:T(8,128)} %copy.37, pred[90]{0:T(512)(128)(4,1)S(1)} %compare_reduce_fusion, f32[16,90,360]{2,0,1:T(8,128)S(1)} %copy-done.2, f32[16,90,360]{2,0,1:T(8,128)} %param.6, f32[32,90,360]{2,0,1:T(8,128)} %bitcast), kind=kLoop, calls=%fused_computation.17 | loop fusion | flops 6220800 | bytes 24883290 | tf_op jit(solution)/shard_map/jit(_where)/select_n | solution.py:67
  423.1 3.4 copy.38
  426.6 3.4 collective-permute-start
  434.1 3.3 collective-permute-start.2
  437.5 4.8 %collective-permute-start.3 = (f32[64,1,360]{2,0,1:T(8,128)}, f32[64,1,360]{2,0,1:T(8,128)}, u32[]{:S(2)}, u32[]{:S(2)}) collective-permute-start(f32[64,1,360]{2,0,1:T(8,128)} %get-tuple-element.8), channel_id=1, source_target_pairs={{0,8},{8,16},{16,24},{24,32},{32,40},{40,48},{48,56},{56,64},{64,7... | collective-permute-start | bytes 276488 | tf_op jit(solution)/shard_map/ppermute | solution.py:17
  445.1 4.6 copy.41
  449.7 4.4 fusion.49
  456.2 4.7 fusion.64
  460.9 6.4 %fusion.45 = (f32[16,90,360]{2,0,1:T(8,128)}, f32[1,16,90,360]{3,1,2,0:T(8,128)S(1)}) fusion(f32[16,92,360]{2,0,1:T(8,128)S(1)} %fusion.17, f32[16,90,362]{2,0,1:T(8,128)S(1)} %fusion.49, f32[64,90,360]{2,0,1:T(8,128)S(1)} %bitcast.28, f32[90]{0:T(128)S(1)} %get-tuple-element.14, f32[90]{0:T(128)S(1)} %get-tuple-element.13, ...), kind=kLoop, calls=%fused_computation.70 | loop fusion | flops 16070400 | bytes 34567168 | tf_op jit(solution)/shard_map/sub | solution.py:91
  469.7 4.4 fusion.53
  (39 shorter events, 19.1 us)
Async XLA Ops:
  0.6 5.2 %copy-start.3 = (f32[16,90,360]{2,0,1:T(8,128)S(1)}, f32[16,90,360]{2,0,1:T(8,128)}, u32[]{:S(2)}) copy-start(f32[16,90,360]{2,0,1:T(8,128)} %param.6) | copy-start | bytes 6220804
  0.6 5.2 %copy-start.2 = (f32[16,90,360]{2,0,1:T(8,128)S(1)}, f32[16,90,360]{2,0,1:T(8,128)}, u32[]{:S(2)}) copy-start(f32[16,90,360]{2,0,1:T(8,128)} %param.7) | copy-start | bytes 6220804
  17.4 5.5 %copy-start.4 = (s32[480]{0:T(512)S(1)}, s32[480]{0:T(512)}, u32[]{:S(2)}) copy-start(s32[480]{0:T(512)} %param.8) | copy-start | bytes 5764
  17.4 5.5 %copy-start.5 = (s32[480]{0:T(512)S(1)}, s32[480]{0:T(512)}, u32[]{:S(2)}) copy-start(s32[480]{0:T(512)} %param.9) | copy-start | bytes 5764
  17.4 110.2 %all-to-all-start = ((f32[64,90,360]{2,1,0:T(8,128)}), f32[64,90,360]{2,1,0:T(8,128)}, u32[]{:S(2)}, u32[]{:S(2)}) async-start(f32[64,90,360]{2,1,0:T(8,128)} %copy.32), calls=%async_computation | async-start | bytes 18874368 | tf_op jit(solution)/shard_map/all_to_all | solution.py:52
  266.4 134.4 %all-to-all-start.1 = ((f32[8,90,2880]{1,0,2:T(8,128)}), f32[8,90,2880]{1,0,2:T(8,128)}, u32[]{:S(2)}, u32[]{:S(2)}) async-start(f32[8,90,2880]{1,0,2:T(8,128)} %copy.35), calls=%async_computation.1 | async-start | bytes 23592960 | tf_op jit(solution)/shard_map/all_to_all | solution.py:54
  418.8 4.3 copy-start
  426.6 15.7 %collective-permute-start = (f32[64,90,1]{1,0,2:T(8,128)S(1)}, f32[64,90,1]{1,0,2:T(8,128)S(1)}, u32[]{:S(2)}, u32[]{:S(2)}) collective-permute-start(f32[64,90,1]{1,0,2:T(8,128)S(1)} %copy.38), channel_id=1, source_target_pairs={{1,0},{2,1},{3,2},{4,3},{5,4},{6,5},{7,6},{0,7},{9,8},{10,9},{11,1... | collective-permute-start | bytes 69128 | tf_op jit(solution)/shard_map/ppermute | solution.py:19
  432.5 12.6 %collective-permute-start.1 = (f32[64,90,1]{1,0,2:T(8,128)}, f32[64,90,1]{1,0,2:T(8,128)}, u32[]{:S(2)}, u32[]{:S(2)}) collective-permute-start(f32[64,90,1]{1,0,2:T(8,128)} %copy.40), channel_id=1, source_target_pairs={{0,1},{1,2},{2,3},{3,4},{4,5},{5,6},{6,7},{7,0},{8,9},{9,10},{10,1... | collective-permute-start | bytes 69128 | tf_op jit(solution)/shard_map/ppermute | solution.py:17
  434.1 20.0 %collective-permute-start.2 = (f32[64,1,360]{2,0,1:T(8,128)}, f32[64,1,360]{2,0,1:T(8,128)S(1)}, u32[]{:S(2)}, u32[]{:S(2)}) collective-permute-start(f32[64,1,360]{2,0,1:T(8,128)} %get-tuple-element.7), channel_id=1, source_target_pairs={{8,0},{16,8},{24,16},{32,24},{40,32},{48,40},{56,48},{64,56},{72,6... | collective-permute-start | bytes 276488 | tf_op jit(solution)/shard_map/ppermute | solution.py:19
  437.5 16.7 %collective-permute-start.3 = (f32[64,1,360]{2,0,1:T(8,128)}, f32[64,1,360]{2,0,1:T(8,128)}, u32[]{:S(2)}, u32[]{:S(2)}) collective-permute-start(f32[64,1,360]{2,0,1:T(8,128)} %get-tuple-element.8), channel_id=1, source_target_pairs={{0,8},{8,16},{16,24},{24,32},{32,40},{40,48},{48,56},{56,64},{64,7... | collective-permute-start | bytes 276488 | tf_op jit(solution)/shard_map/ppermute | solution.py:17
  445.1 9.1 %slice-start = ((s8[8847360]{0:T(1024)(128)(4,1)}), s8[458752]{0:T(1024)(128)(4,1)S(1)}, s32[]{:S(2)}) async-start(s8[8847360]{0:T(1024)(128)(4,1)} %bitcast.27), calls=%async_computation.2 | async-start | bytes 917504
  449.7 4.5 slice-start.1
  449.7 5.3 %slice-start.2 = ((s8[8847360]{0:T(1024)(128)(4,1)}), s8[4194304]{0:T(1024)(128)(4,1)S(1)}, s32[]{:S(2)}) async-start(s8[8847360]{0:T(1024)(128)(4,1)} %bitcast.27), calls=%async_computation.4 | async-start | bytes 8388608
  454.2 2.0 copy-start.1
where the time goes:
time: 481 us; the launch traced here: 474 us
  waiting for transfers between devices  160 us (33%)
  other arithmetic  107 us (22%)
  matrix products  105 us (22%)
  local copies, waits for them, and re-layouts  79.9 us (17%)
  starting transfers between devices  22.3 us (5%)
    all_to_all x1, waiting for transfers between devices, filter_rows(): lax.all_to_all(smooth, 'lon', split_axis=2, concat_axis=0, tiled=True)  129 us
    dot_general x1, matrix products, truncate_rows(): spec = jnp.einsum('pqn,nk->pqk', rows, forward, precision=HIGH)  53.3 us
    dot_general x1, matrix products, truncate_rows(): return jnp.einsum('pqk,kn->pqn', spec, inverse, precision=HIGH)  51.3 us
    mul x1, other arithmetic, truncate_rows(): jnp.cos(angle) * weight[None, :]  36.9 us
    sin x1, other arithmetic, truncate_rows(): forward = jnp.concatenate([jnp.cos(angle), jnp.sin(angle)], axis=1)  36.6 us
    all_to_all x1, waiting for transfers between devices, filter_rows(): lax.all_to_all(stacked, 'lon', split_axis=0, concat_axis=2, tiled=True)  30.7 us
    all_to_all x2, local copies, waits for them, and re-layouts, filter_rows(): lax.all_to_all(stacked, 'lon', split_axis=0, concat_axis=2, tiled=True)  22.7 us
    all_to_all x1, local copies, waits for them, and re-layouts, filter_rows(): lax.all_to_all(smooth, 'lon', split_axis=2, concat_axis=0, tiled=True)  11.6 us
  transfers between devices with their start and end apart: 6, of which 2 were waited for; matrix products, arithmetic and copies ran while one was open for 19% of the time, Pallas kernels for 0%

commit v1 on v0

v1 whole, which is shorter than its diff:
```python
import functools

import jax
import jax.numpy as jnp
import numpy as np
from jax import lax
from jax.experimental import pallas as pl
from jax.experimental.pallas import tpu as pltpu
from jax.sharding import PartitionSpec as P

NLON = 2880
NLAT = 1440
LEV = 16
ROWS = 90
COLS = 360
PR = 96
PC = 384
NP = 8
FIELDS = 64
NCH = 4
CF = 2
NOFF = 0
SHIFT = 6
MESH = pl.DeviceIdType.MESH
F32 = jnp.float32
BF16 = jnp.bfloat16


def split(table):
    hi = table.astype(np.float32).astype(BF16)
    lo = (table - hi.astype(np.float64)).astype(np.float32).astype(BF16)
    return np.asarray(hi), np.asarray(lo)


@functools.lru_cache(maxsize=None)
def value_tables():
    q = np.arange(PC)
    q = np.where(q == PC - 1, -1, q)
    forward = np.zeros((4, 2 * PC, PC))
    inverse = np.zeros((4, PC, 2 * PC))
    waves = np.full((4, PC), 1e9)
    m = np.arange(90)
    for g in range(4):
        parts = [(0, 0, 0), (4, 1, 0)] if g == 0 else [(g, 0, 1), (8 - g, 0, -1)]
        for slot, (r, half, sign) in enumerate(parts):
            k = 8 * m + r
            angle = 2.0 * np.pi * ((k[:, None] * q[None, :]) % NLON) / NLON
            cos, sin = np.cos(angle), np.sin(angle)
            re = slice(slot * 180, slot * 180 + 90)
            im = slice(slot * 180 + 90, slot * 180 + 180)
            waves[g, re] = k
            waves[g, im] = k
            weight = np.where(k == 0, 1.0, 2.0)[:, None] / NLON
            own = np.zeros((PC, 2 * PC))
            if sign == 0:
                own[re, half * PC : (half + 1) * PC] = cos
                own[im, half * PC : (half + 1) * PC] = -sin
            else:
                own[re, :PC] = cos
                own[im, :PC] = -sin
                own[re, PC:] = sign * sin
                own[im, PC:] = sign * cos
            scaled = own.copy()
            scaled[re] *= weight
            scaled[im] *= weight
            inverse[g] += scaled
            keep = np.concatenate([np.arange(PC) < COLS] * 2)
            forward[g] += (own * keep[None, :]).T
    used = np.concatenate([(np.arange(PC) <= COLS) | (np.arange(PC) == PC - 1)] * 2)
    inverse = inverse * used[None, None, :]
    return split(forward) + split(inverse) + (waves.astype(np.float32),)


@functools.lru_cache(maxsize=None)
def packed_tables():
    lane = np.arange(PC)
    wave = (lane + 1) // 2
    is_cos = (lane == 0) | (lane % 2 == 1)
    q = np.arange(PC)
    q = np.where(q == PC - 1, -1, q)
    used = (np.arange(PC) <= COLS) | (np.arange(PC) == PC - 1)
    forward = np.zeros((NP, 2, PC, PC))
    inverse = np.zeros((NP, 2, PC, PC))
    for p in range(NP):
        n = COLS * p + q
        angle = 2.0 * np.pi * ((wave[:, None] * n[None, :]) % NLON) / NLON
        base = np.where(is_cos[:, None], np.cos(angle), np.sin(angle))
        weight = np.where(wave == 0, 1.0, 2.0)[:, None] / NLON
        back = base * weight * used[None, :]
        ahead = (base * (np.arange(PC) < COLS)[None, :]).T
        forward[p, 0], forward[p, 1] = ahead, ahead[:, ::-1]
        inverse[p, 0], inverse[p, 1] = back, back[::-1]
    waves = np.stack([wave, wave[::-1]]).astype(np.float32)
    return split(forward) + split(inverse) + (waves,)


def dot3(x, hi, lo):
    x_hi = x.astype(BF16)
    x_lo = (x - x_hi.astype(F32)).astype(BF16)
    total = jnp.dot(x_hi, lo, preferred_element_type=F32)
    total += jnp.dot(x_lo, hi, preferred_element_type=F32)
    return total + jnp.dot(x_hi, hi, preferred_element_type=F32)


def filter_kernel(
    w_ref, t_ref, h_ref, lim_ref, own_ref, wv_ref, wp_ref,
    thi_ref, tlo_ref, uhi_ref, ulo_ref, fhi_ref, flo_ref, ghi_ref, glo_ref,
    filt_ref, side_ref, edge_ref,
    thi, tlo, uhi, ulo, fhi, flo, ghi, glo,
    recv, ret, srecv, stage, xs, obuf, yb, zb, cols, rawedge, fedge, sedge,
    tab_sem, stage_sem, fsend, frecv, rsend, rrecv, ssend, srecv_sem, asend, arecv,
    hsend, hrecv, lsend, lrecv, esem, osem,
):
    lat = lax.axis_index("lat")
    lon = lax.axis_index("lon")
    north = lat < 8
    depth = jnp.where(north, lat, 15 - lat)
    partner = jnp.where(north, jnp.where(lat < 4, lat + 4, lat - 4), jnp.where(lat >= 12, lat - 4, lat + 4))
    is_packed = depth == 0
    is_value = (depth >= 1) & (depth <= 3)
    is_off = (depth >= 5) & (depth <= 7)
    served = jnp.where(is_off, partner, lat)
    fields_of = ((w_ref, 0, 4), (t_ref, 4, 2), (h_ref, 6, 2))

    bar = pltpu.get_barrier_semaphore()
    for i in range(1, NP):
        pl.semaphore_signal(bar, inc=1, device_id=(lat, lax.rem(lon + i, NP)), device_id_type=MESH)
    for i in (1, 15):
        pl.semaphore_signal(bar, inc=1, device_id=(lax.rem(lat + i, 16), lon), device_id_type=MESH)
    n_signals = 9
    if NOFF:
        for i in range(NP):
            pl.semaphore_signal(bar, inc=1, device_id=(partner, lax.rem(lon + i, NP)), device_id_type=MESH)
        n_signals += 8

    tables = ((thi_ref, thi), (tlo_ref, tlo), (uhi_ref, uhi), (ulo_ref, ulo))
    packs = ((fhi_ref, fhi), (flo_ref, flo), (ghi_ref, ghi), (glo_ref, glo))

    @pl.when(is_value | is_off)
    def _():
        for i, (src, dst) in enumerate(tables):
            pltpu.make_async_copy(src, dst, tab_sem.at[i]).start()

    @pl.when(is_packed)
    def _():
        for i, (src, dst) in enumerate(packs):
            pltpu.make_async_copy(src.at[lon], dst, tab_sem.at[i]).start()

    def stage_copy(g, slot):
        src, lo, _ = fields_of[0 if g < 4 else 1 if g < 6 else 2]
        return pltpu.make_async_copy(src.at[pl.ds((g - lo) * 8, 8)], stage.at[slot], stage_sem.at[slot])

    stage_copy(0, 0).start()
    xs[...] = jnp.zeros_like(xs)
    yb[...] = jnp.zeros_like(yb)
    cols[...] = jnp.zeros_like(cols)

    pl.semaphore_wait(bar, n_signals)

    def variants(fn):
        @pl.when((served != 3) & (served != 12))
        def _():
            fn(0, ROWS, PR)

        @pl.when(served == 3)
        def _():
            fn(0, 32, 32)

        @pl.when(served == 12)
        def _():
            fn(56, ROWS - 56, PR - 56)

    @pl.when(is_value)
    def _():
        def per_rows(r0, rn, _):
            def per_copy(n, carry):
                c = n // NP
                p = lax.rem(lon + n, NP)
                target = jnp.where(c < NOFF, partner, lat)
                local = (c >= NOFF) & (p == lon)
                for arr, lo, cnt in fields_of:
                    mine = (p >= lo) & (p < lo + cnt)
                    src = arr.at[pl.ds((p - lo) * 8 + c * CF, CF), r0 : r0 + rn]
                    dst = recv.at[c, lon, :, r0 : r0 + rn]

                    @pl.when(mine & jnp.logical_not(local))
                    def _():
                        pltpu.make_async_remote_copy(
                            src_ref=src, dst_ref=dst, send_sem=fsend.at[c, p],
                            recv_sem=frecv.at[c, lon], device_id=(target, p), device_id_type=MESH,
                        ).start()

                    @pl.when(mine & local)
                    def _():
                        pltpu.make_async_copy(src, dst, frecv.at[c, lon]).start()

                return carry

            lax.fori_loop(0, NCH * NP, per_copy, 0)

        variants(per_rows)

    @pl.when(is_packed)
    def _():
        for i, (src, dst) in enumerate(packs):
            pltpu.make_async_copy(src.at[lon], dst, tab_sem.at[i]).wait()

    lane = lax.broadcasted_iota(jnp.int32, (ROWS, 128), 1)

    def strips_to(g, dst_lon, slot):
        return pltpu.make_async_remote_copy(
            src_ref=ret.at[pl.ds(g * 8, 8), 0:48], dst_ref=srecv.at[pl.ds(slot * 8, 8)],
            send_sem=ssend.at[g], recv_sem=srecv_sem.at[slot],
            device_id=(lat, dst_lon), device_id_type=MESH,
        )

    for g in range(NP):
        slot = g % 2
        if g + 1 < NP:
            stage_copy(g + 1, 1 - slot).start()
        stage_copy(g, slot).wait()

        def columns(f, carry, g=g, slot=slot):
            at = g * 8 + f
            block = stage[slot, f]
            cur = cols[0:ROWS, :]
            cur = jnp.where(lane == at, block[:, 0:1], cur)
            cur = jnp.where(lane == at + FIELDS, block[:, COLS - 1 : COLS], cur)
            cols[0:ROWS, :] = cur
            return carry

        lax.fori_loop(0, 8, columns, 0)
        for f in range(8):
            rawedge[0, g * 8 + f : g * 8 + f + 1, 0:COLS] = stage[slot, f, 0:1, :]
            rawedge[1, g * 8 + f : g * 8 + f + 1, 0:COLS] = stage[slot, f, ROWS - 1 : ROWS, :]

        @pl.when(is_packed)
        def _(g=g, slot=slot):
            @pl.when(north)
            def _():
                xs[:, SHIFT : SHIFT + ROWS, 0:COLS] = stage[slot]

            @pl.when(jnp.logical_not(north))
            def _():
                xs[:, 0:ROWS, 0:COLS] = stage[slot]

            low = dot3(xs[:, 0:48, :].reshape(8 * 48, PC), fhi[0], flo[0]).reshape(8, 48, PC)
            high = dot3(xs[:, 48:96, :].reshape(8 * 48, PC), fhi[1], flo[1]).reshape(8, 48, PC)
            keep_low = wp_ref[0:1, :] <= lim_ref[0:48, 0:1]
            keep_high = wp_ref[1:2, :] <= lim_ref[48:96, 0:1]
            low = jnp.where(keep_low[None], low, 0.0)
            high = jnp.where(keep_high[None], high, 0.0)
            for t in range(6):
                ret[g * 8 : g * 8 + 8, 8 * t : 8 * t + 8, :] = (
                    low[:, 8 * t : 8 * t + 8, :] + high[:, 40 - 8 * t : 48 - 8 * t, :]
                )

            @pl.when(lon != g)
            def _():
                strips_to(g, g, lon).start()

            @pl.when(lon == g)
            def _():
                pltpu.make_async_copy(
                    ret.at[pl.ds(g * 8, 8), 0:48], srecv.at[pl.ds(g * 8, 8)], srecv_sem.at[g]
                ).start()

    def side_copy(i):
        step = 1 if i == 0 else NP - 1
        return pltpu.make_async_remote_copy(
            src_ref=cols, dst_ref=side_ref.at[i], send_sem=hsend.at[i], recv_sem=hrecv.at[i],
            device_id=(lat, lax.rem(lon + step, NP)), device_id_type=MESH,
        )

    side_copy(0).start()
    side_copy(1).start()

    @pl.when(is_packed)
    def _():
        def wait_part(s, carry):
            pltpu.make_async_copy(
                srecv.at[pl.ds(s * 8, 8)], srecv.at[pl.ds(s * 8, 8)], srecv_sem.at[s]
            ).wait()
            return carry

        lax.fori_loop(0, NP, wait_part, 0)

        def add(f, carry):
            total = srecv[f]
            for s in range(1, NP):
                total = total + srecv[s * 8 + f]
            ret[lon * 8 + f, 48:96, :] = total
            return carry

        lax.fori_loop(0, 8, add, 0)

        def sum_to(p):
            return pltpu.make_async_remote_copy(
                src_ref=ret.at[pl.ds(lon * 8, 8), 48:96], dst_ref=ret.at[pl.ds(lon * 8, 8), 48:96],
                send_sem=asend.at[p], recv_sem=arecv.at[lon],
                device_id=(lat, p), device_id_type=MESH,
            )

        def send(i, carry):
            sum_to(lax.rem(lon + i, NP)).start()
            return carry

        lax.fori_loop(1, NP, send, 0)

        def out_copy(g, slot):
            return pltpu.make_async_copy(obuf.at[slot], filt_ref.at[pl.ds(g * 8, 8)], osem.at[slot])

        def back(i, carry):
            g = lax.rem(lon + i, NP)
            slot = lax.rem(i, 2)

            @pl.when(i > 0)
            def _():
                pltpu.make_async_copy(
                    ret.at[pl.ds(g * 8, 8), 48:96], ret.at[pl.ds(g * 8, 8), 48:96], arecv.at[g]
                ).wait()

            @pl.when(i >= 2)
            def _():
                out_copy(g, slot).wait()

            spec = ret[pl.ds(g * 8, 8), 48:96, :]
            keep_low = wp_ref[0:1, :] <= lim_ref[0:48, 0:1]
            low = jnp.where(keep_low[None], spec, 0.0).reshape(8 * 48, PC)
            low = dot3(low, ghi[0], glo[0]).reshape(8, 48, PC)
            keep_high = wp_ref[1:2, :] <= lim_ref[48:96, 0:1]
            flipped = jnp.concatenate([spec[:, 40 - 8 * t : 48 - 8 * t, :] for t in range(6)], axis=1)
            high = jnp.where(keep_high[None], flipped, 0.0).reshape(8 * 48, PC)
            high = dot3(high, ghi[1], glo[1]).reshape(8, 48, PC)

            @pl.when(north)
            def _():
                obuf[slot, :, 0 : 48 - SHIFT, :] = low[:, SHIFT:48, :]
                obuf[slot, :, 48 - SHIFT : ROWS, :] = high

            @pl.when(jnp.logical_not(north))
            def _():
                obuf[slot, :, 0:48, :] = low
                obuf[slot, :, 48:96, :] = high

            out_copy(g, slot).start()
            return carry

        lax.fori_loop(0, NP, back, 0)
        for slot in range(2):
            out_copy(0, slot).wait()

        def sent(i, carry):
            p = lax.rem(lon + i, NP)
            sum_to(p).wait_send()
            strips_to(p, p, lon).wait_send()
            return carry

        lax.fori_loop(1, NP, sent, 0)

    @pl.when(is_value | is_off)
    def _():
        for i, (src, dst) in enumerate(tables):
            pltpu.make_async_copy(src, dst, tab_sem.at[i]).wait()

        first = jnp.where(is_off, 0, NOFF)
        last = jnp.where(is_off, NOFF, NCH)
        half = np.float32(np.sqrt(0.5))

        def chunk(c, carry):
            def arrived(r0, rn, _):
                def wait_one(s, carry):
                    ref = recv.at[c, s, :, r0 : r0 + rn]
                    pltpu.make_async_copy(ref, ref, frecv.at[c, s]).wait()
                    return carry

                lax.fori_loop(0, NP, wait_one, 0)

            variants(arrived)

            def fold(f, carry):
                row0 = pl.multiple_of(f * PR, PR)
                rows = pl.ds(row0, ROWS)
                x = [recv[c, s, f] for s in range(NP)]
                s0, s1, s2, s3 = [x[j] + x[j + 4] for j in range(4)]
                d0, d1, d2, d3 = [x[j] - x[j + 4] for j in range(4)]
                plus, minus = half * (d1 + d3), half * (d1 - d3)
                out = (
                    (s0 + s2) + (s1 + s3), (s0 + s2) - (s1 + s3),
                    d0 + minus, -(d2 + plus),
                    s0 - s2, s3 - s1,
                    d0 - minus, d2 - plus,
                )
                for i in range(8):
                    yb[i, rows, 0:COLS] = out[i]
                return carry

            lax.fori_loop(0, CF, fold, 0)

            def group(g, carry):
                spec = dot3(yb[2 * g], thi[g, 0:PC, :], tlo[g, 0:PC, :])
                spec += dot3(yb[2 * g + 1], thi[g, PC:, :], tlo[g, PC:, :])
                keep = wv_ref[g] <= lim_ref[:, 0:1]
                spec = jnp.where(keep[None], spec.reshape(CF, PR, PC), 0.0).reshape(CF * PR, PC)
                zb[2 * g] = dot3(spec, uhi[g, :, 0:PC], ulo[g, :, 0:PC])
                zb[2 * g + 1] = dot3(spec, uhi[g, :, PC:], ulo[g, :, PC:])
                return carry

            lax.fori_loop(0, 4, group, 0)

            def unfold(f, carry):
                rows = pl.ds(pl.multiple_of(f * PR, PR), PR)
                a0, b0, a1, b1, a2, b2, a3, b3 = [zb[i, rows, :] for i in range(8)]
                even = (a0 + b0 + a2, a0 - b0 - b2, a0 + b0 - a2, a0 - b0 + b2)
                odd = (a1 + a3, half * ((a1 - a3) - (b1 + b3)), b3 - b1, half * ((a3 - a1) - (b1 + b3)))
                for j in range(4):
                    ret[(c * NP + j) * CF + f] = even[j] + odd[j]
                    ret[(c * NP + j + 4) * CF + f] = even[j] - odd[j]
                return carry

            lax.fori_loop(0, CF, unfold, 0)

            def give_back(r0, _, rn):
                def one(i, carry):
                    p = lax.rem(lon + i, NP)
                    src = ret.at[pl.ds((c * NP + p) * CF, CF), r0 : r0 + rn]
                    dst = filt_ref.at[pl.ds(lon * 8 + c * CF, CF), r0 : r0 + rn]
                    local = is_value & (p == lon)

                    @pl.when(jnp.logical_not(local))
                    def _():
                        pltpu.make_async_remote_copy(
                            src_ref=src, dst_ref=dst, send_sem=rsend.at[c, p],
                            recv_sem=rrecv.at[c, lon], device_id=(served, p), device_id_type=MESH,
                        ).start()

                    @pl.when(local)
                    def _():
                        pltpu.make_async_copy(src, dst, rrecv.at[c, lon]).start()

                    return carry

                lax.fori_loop(0, NP, one, 0)

            variants(give_back)
            return carry

        lax.fori_loop(first, last, chunk, 0)

        def drain_returns(r0, _, rn):
            def one(n, carry):
                c = first + n // NP
                p = lax.rem(n, NP)
                src = ret.at[pl.ds((c * NP + p) * CF, CF), r0 : r0 + rn]

                @pl.when(jnp.logical_not(is_value & (p == lon)))
                def _():
                    pltpu.make_async_copy(src, src, rsend.at[c, p]).wait()

                return carry

            lax.fori_loop(0, (last - first) * NP, one, 0)

        variants(drain_returns)

    @pl.when(is_value)
    def _():
        def drain(r0, rn, rb):
            def one(n, carry):
                c = n // NP
                p = lax.rem(n, NP)
                src = recv.at[c, p, :, r0 : r0 + rn]
                dst = filt_ref.at[pl.ds(p * 8 + c * CF, CF), r0 : r0 + rb]

                @pl.when((c < NOFF) | (p != lon))
                def _():
                    pltpu.make_async_copy(src, src, fsend.at[c, p]).wait()

                pltpu.make_async_copy(dst, dst, rrecv.at[c, p]).wait()
                return carry

            lax.fori_loop(0, NCH * NP, one, 0)

        variants(drain)

    sedge[...] = rawedge[...]

    @pl.when(depth <= 3)
    def _():
        for i, r0 in enumerate((0, 88)):
            pltpu.make_async_copy(filt_ref.at[:, r0 : r0 + 8], fedge.at[i], esem.at[i]).start()
        for i, (r0, row) in enumerate(((0, 0), (88, ROWS - 1))):
            pltpu.make_async_copy(filt_ref.at[:, r0 : r0 + 8], fedge.at[i], esem.at[i]).wait()
            keep = own_ref[row : row + 1, 0:1] >= 0.0
            for f in range(FIELDS):
                sedge[i, f : f + 1, :] = jnp.where(
                    keep, fedge[i, f, row - r0 : row - r0 + 1, :], rawedge[i, f : f + 1, :]
                )

    def edge_copy(i):
        step = 15 if i == 0 else 1
        return pltpu.make_async_remote_copy(
            src_ref=sedge.at[i], dst_ref=edge_ref.at[i], send_sem=lsend.at[i], recv_sem=lrecv.at[i],
            device_id=(lax.rem(lat + step, 16), lon), device_id_type=MESH,
        )

    edge_copy(0).start()
    edge_copy(1).start()
    side_copy(0).wait()
    side_copy(1).wait()
    edge_copy(0).wait()
    edge_copy(1).wait()


def stencil_kernel(
    u_ref, v_ref, t_ref, h_ref, fu_ref, fv_ref, ft_ref, fh_ref, side_ref, edge_ref, row_ref,
    wind_out, t_out, h_out, st,
):
    level = pl.program_id(0)
    lat = lax.axis_index("lat")
    listed = row_ref[0, :, 0:1] >= 0.0
    lane = lax.broadcasted_iota(jnp.int32, (PR, 128), 1)
    row = lax.broadcasted_iota(jnp.int32, (PR, PC), 0)
    has_north = lat > 0
    has_south = lat < 15
    state = []
    for k, (raw, smooth) in enumerate(((u_ref, fu_ref), (v_ref, fv_ref), (t_ref, ft_ref), (h_ref, fh_ref))):
        f = k * LEV + level
        st[k, 0:ROWS, 0:COLS] = raw[0]
        east = jnp.sum(jnp.where(lane == f, side_ref[1], 0.0), axis=1, keepdims=True)
        west = jnp.sum(jnp.where(lane == f + FIELDS, side_ref[0], 0.0), axis=1, keepdims=True)
        tail = st[k, :, 256:PC]
        tail = jnp.where(lane == COLS - 256, east, tail)
        tail = jnp.where(lane == 127, west, tail)
        st[k, :, 256:PC] = tail
        field = jnp.where(listed, smooth[0], st[k])
        above = jnp.where(has_north, edge_ref[1, pl.ds(f, 1), :], 0.0)
        below = jnp.where(has_south, edge_ref[0, pl.ds(f, 1), :], 0.0)
        field = jnp.where(row == ROWS, below, field)
        field = jnp.where(row == PR - 1, above, field)
        state.append(field)
    u, v, t, h = state
    cos = row_ref[1, :, 0:1]
    inv = row_ref[2, :, 0:1]
    sin = row_ref[3, :, 0:1]

    def dx(a):
        return (pltpu.roll(a, PC - 1, 1) - pltpu.roll(a, 1, 1)) * 0.5

    def dy(a):
        return (pltpu.roll(a, PR - 1, 0) - pltpu.roll(a, 1, 0)) * 0.5

    cu = 0.05 * u * inv
    cv = 0.2 * v
    new_h = h - (0.05 * inv) * dx(u * h) - (0.2 * inv) * dy(v * h * cos)
    new_t = t - cu * dx(t) - cv * dy(t)
    new_u = u - cu * dx(u) - cv * dy(u) - (0.1 * inv) * dx(h) + (0.3 * sin) * v
    new_v = v - cu * dx(v) - cv * dy(v) - 0.3 * dy(h) - (0.3 * sin) * u
    wind_out[0, 0] = new_u[0:ROWS, 0:COLS]
    wind_out[1, 0] = new_v[0:ROWS, 0:COLS]
    t_out[0] = new_t[0:ROWS, 0:COLS]
    h_out[0] = new_h[0:ROWS, 0:COLS]


def limits(first_row, polar_rows, cutoffs):
    rows = first_row + jnp.arange(PR, dtype=jnp.int32)
    hits = polar_rows[None, :] == rows[:, None]
    limit = jnp.max(jnp.where(hits, cutoffs[None, :], -1), axis=1).astype(F32)
    return jnp.broadcast_to(limit[:, None], (PR, 128))


def body(winds, theta, thick, polar_rows, cutoffs):
    lat = lax.axis_index("lat")
    served = jnp.where((lat >= 4) & (lat < 8), lat - 4, jnp.where((lat >= 8) & (lat < 12), lat + 4, lat))
    shift = jnp.where(lat == 0, SHIFT, 0)
    lim = limits(served * ROWS - shift, polar_rows, cutoffs)
    own = limits(lat * ROWS, polar_rows, cutoffs)
    thi, tlo, uhi, ulo, wv = value_tables()
    fhi, flo, ghi, glo, wp = packed_tables()
    vm = pl.BlockSpec(memory_space=pltpu.VMEM)
    hbm = pl.BlockSpec(memory_space=pl.ANY)
    dma = pltpu.SemaphoreType.DMA
    filt, side, edge = pl.pallas_call(
        filter_kernel,
        out_shape=(
            jax.ShapeDtypeStruct((FIELDS, PR, PC), F32),
            jax.ShapeDtypeStruct((2, PR, 128), F32),
            jax.ShapeDtypeStruct((2, FIELDS, PC), F32),
        ),
        in_specs=[hbm, hbm, hbm, vm, vm, vm, vm] + [hbm] * 8,
        out_specs=(hbm, hbm, hbm),
        scratch_shapes=[
            pltpu.VMEM((4, 2 * PC, PC), BF16), pltpu.VMEM((4, 2 * PC, PC), BF16),
            pltpu.VMEM((4, PC, 2 * PC), BF16), pltpu.VMEM((4, PC, 2 * PC), BF16),
            pltpu.VMEM((2, PC, PC), BF16), pltpu.VMEM((2, PC, PC), BF16),
            pltpu.VMEM((2, PC, PC), BF16), pltpu.VMEM((2, PC, PC), BF16),
            pltpu.VMEM((NCH, NP, CF, ROWS, COLS), F32),
            pltpu.VMEM((FIELDS, PR, PC), F32),
            pltpu.VMEM((FIELDS, 48, PC), F32),
            pltpu.VMEM((2, 8, ROWS, COLS), F32),
            pltpu.VMEM((8, PR, PC), F32),
            pltpu.VMEM((2, 8, PR, PC), F32),
            pltpu.VMEM((8, CF * PR, PC), F32),
            pltpu.VMEM((8, CF * PR, PC), F32),
            pltpu.VMEM((PR, 128), F32),
            pltpu.VMEM((2, FIELDS, PC), F32),
            pltpu.VMEM((2, FIELDS, 8, PC), F32),
            pltpu.VMEM((2, FIELDS, PC), F32),
            dma((4,)), dma((2,)),
            dma((NCH, NP)), dma((NCH, NP)), dma((NCH, NP)), dma((NCH, NP)),
            dma((NP,)), dma((NP,)), dma((NP,)), dma((NP,)),
            dma((2,)), dma((2,)), dma((2,)), dma((2,)), dma((2,)), dma((2,)),
        ],
        compiler_params=pltpu.CompilerParams(
            collective_id=1, has_side_effects=True, vmem_limit_bytes=58 * 2**20
        ),
        name="polar_filter",
    )(
        winds.reshape(2 * LEV, ROWS, COLS), theta, thick, lim, own,
        jnp.asarray(wv)[:, None, :], jnp.asarray(wp), thi, tlo, uhi, ulo, fhi, flo, ghi, glo,
    )

    rows = jnp.arange(PR, dtype=jnp.int32)
    rows = lat * ROWS + jnp.where(rows == PR - 1, -1, rows)
    angle = (rows.astype(F32) + 0.5) * (jnp.pi / NLAT)
    cos, sin = jnp.sin(angle), -jnp.cos(angle)
    trig = jnp.stack([cos, 1.0 / cos, sin])
    row_info = jnp.concatenate([own[None], jnp.broadcast_to(trig[:, :, None], (3, PR, 128))], axis=0)

    def raw(block):
        return pl.BlockSpec((1, ROWS, COLS), lambda l: (l + block, 0, 0))

    def smooth(block):
        return pl.BlockSpec((1, PR, PC), lambda l: (l + block, 0, 0))

    def whole(*shape):
        return pl.BlockSpec(shape, lambda l: (0,) * len(shape))

    flat = winds.reshape(2 * LEV, ROWS, COLS)
    return pl.pallas_call(
        stencil_kernel,
        grid=(LEV,),
        out_shape=(
            jax.ShapeDtypeStruct((2, LEV, ROWS, COLS), F32),
            jax.ShapeDtypeStruct((LEV, ROWS, COLS), F32),
            jax.ShapeDtypeStruct((LEV, ROWS, COLS), F32),
        ),
        in_specs=[
            raw(0), raw(LEV), raw(0), raw(0), smooth(0), smooth(LEV), smooth(2 * LEV), smooth(3 * LEV),
            whole(2, PR, 128), whole(2, FIELDS, PC), whole(4, PR, 128),
        ],
        out_specs=(
            pl.BlockSpec((2, 1, ROWS, COLS), lambda l: (0, l, 0, 0)),
            pl.BlockSpec((1, ROWS, COLS), lambda l: (l, 0, 0)),
            pl.BlockSpec((1, ROWS, COLS), lambda l: (l, 0, 0)),
        ),
        scratch_shapes=[pltpu.VMEM((4, PR, PC), F32)],
        compiler_params=pltpu.CompilerParams(vmem_limit_bytes=32 * 2**20),
        name="stencil",
    )(flat, flat, theta, thick, filt, filt, filt, filt, side, edge, row_info)


def solution(mesh):
    in_specs = (P(None, None, "lat", "lon"), P(None, "lat", "lon"), P(None, "lat", "lon"), P(), P())
    out_specs = (P(None, None, "lat", "lon"), P(None, "lat", "lon"), P(None, "lat", "lon"))
    return jax.shard_map(body, mesh=mesh, in_specs=in_specs, out_specs=out_specs, check_vma=False)
```

time: 481 us -> 227 us (0.47); the launches traced: 474 us -> 226 us
  Pallas kernels: 0 us -> 198 us
  waiting for transfers between devices: 160 us -> 0 us
  other arithmetic: 107 us -> 1.07 us
  matrix products: 105 us -> 0 us
  local copies, waits for them, and re-layouts: 79.9 us -> 26.2 us
  starting transfers between devices: 22.3 us -> 0 us
    pallas_call x0 -> x2, Pallas kernels: none -> 198 us  [the longest x1 181 us: body(): pl.pallas_call(filter_kernel, out_shape=(jax.ShapeDtypeStruct((FIELDS, PR...]
    all_to_all x2 -> x0, waiting for transfers between devices: 160 us -> none  [the longest x1 129 us: filter_rows(): lax.all_to_all(smooth, 'lon', split_axis=2, concat_axis=0, tiled=True)]
    dot_general x2 -> x0, matrix products: 105 us -> none  [the longest x1 53.3 us: truncate_rows(): spec = jnp.einsum('pqn,nk->pqk', rows, forward, precision=HIGH)]
    mul x4 -> x0, other arithmetic: 42.5 us -> none  [the longest x1 36.9 us: truncate_rows(): jnp.cos(angle) * weight[None, :]]
    sin x2 -> x1, other arithmetic: 36.6 us -> 0.05 us  [body(): cos, sin = (jnp.sin(angle), -jnp.cos(angle))]
    all_to_all x3 -> x0, local copies, waits for them, and re-layouts: 34.3 us -> none  [the longest x2 22.7 us: filter_rows(): lax.all_to_all(stacked, 'lon', split_axis=0, concat_axis=2, tiled=True)]
    ppermute x4 -> x0, starting transfers between devices: 11.6 us -> none  [the longest x2 6.73 us: padded(): lax.ppermute(head, axis, [((i + 1) % count, i) for i in range(ends)])]
    dot_general x1 -> x0, local copies, waits for them, and re-layouts: 11.4 us -> none  [truncate_rows(): return jnp.einsum('pqk,kn->pqn', spec, inverse, precision=HIGH)]
  transfers between devices with their start and end apart: 6 -> 0, of which waited for: 2 -> 0; matrix products, arithmetic and copies ran while one was open for 19% -> 0% of each run, Pallas kernels for 0% -> 0%
where the time goes in v1:
time: 227 us; the launch traced here: 226 us
  Pallas kernels  198 us (87%)
  local copies, waits for them, and re-layouts  26.2 us (12%)
    pallas_call x1, Pallas kernels, body(): pl.pallas_call(filter_kernel, out_shape=(jax.ShapeDtypeStruct((FIELDS, PR...  181 us
    pallas_call x1, Pallas kernels, body(): pl.pallas_call(stencil_kernel, grid=(LEV,), out_shape=(jax.ShapeDtypeStru...  17 us
    unnamed x21, local copies, waits for them, and re-layouts  14.7 us
    pallas_call x3, local copies, waits for them, and re-layouts, body(): pl.pallas_call(stencil_kernel, grid=(LEV,), out_shape=(jax.ShapeDtypeStru...  9.93 us

profile of v1, /device:TPU:97, one launch (start us, length us, event | category | flops | bytes accessed | tf_op | source)
XLA Modules:
  0.0 226.3 jit_solution(18408615018866599289)
XLA Ops:
  0.7 0.9 select_reduce_fusion
  1.7 0.7 broadcast_in_dim.49.lim_ref
  2.4 0.1 broadcast_in_dim_broadcast_in_dim.2
  2.5 0.7 broadcast_in_dim.50.own_ref
  3.2 0.1 broadcast_in_dim.53
  3.3 0.0 slice-start.2
  3.4 0.0 slice-start.3
  3.4 3.9 %copy.29.t_ref = f32[16,90,360]{2,1,0:T(8,128)} copy(f32[16,90,360]{2,0,1:T(8,128)} %param.16) | data formatting | bytes 4147200 | tf_op args[1]
  7.3 0.0 copy-done.4
  7.3 2.1 copy.30.h_ref
  9.4 0.0 slice-done.2
  9.4 0.0 slice-done.3
  9.4 3.6 %copy.26 = f32[2,16,90,360]{3,2,1,0:T(8,128)} copy(f32[2,16,90,360]{3,1,2,0:T(8,128)S(1)} %bitcast.7) | data formatting | bytes 8294400 | tf_op args[0]
  12.9 181.1 %polar_filter.1 = (f32[64,96,384]{2,1,0:T(8,128)}, f32[2,96,128]{2,1,0:T(8,128)}, f32[2,64,384]{2,1,0:T(8,128)}) custom-call(f32[32,90,360]{2,1,0:T(8,128)} %bitcast.1, f32[16,90,360]{2,1,0:T(8,128)} %copy.29.t_ref, f32[16,90,360]{2,1,0:T(8,128)} %copy.30.h_ref, f32[96,128]{1,0:T(8,128)} %broadcast_in_dim.49.lim_ref, f32[96,128]{1,0:T(8,128)} %broadcast_in_dim.50.own_ref, ...), custom_call_target="tpu_custom_call" | custom-call | tf_op jit(solution)/shard_map/polar_filter/pallas_call | solution.py:583
  194.1 0.0 slice-done
  194.1 0.0 copy-start
  194.1 1.7 copy-done
  195.8 1.7 copy-done.1
  197.5 0.9 copy-done.2
  198.4 0.9 copy-done.3
  199.3 17.0 %stencil.1 = (f32[2,16,90,360]{3,2,1,0:T(8,128)S(1)}, f32[16,90,360]{2,1,0:T(8,128)S(1)}, f32[16,90,360]{2,1,0:T(8,128)S(1)}) custom-call(f32[32,90,360]{2,1,0:T(8,128)S(1)} %bitcast.4, f32[32,90,360]{2,1,0:T(8,128)S(1)} %bitcast.5, f32[16,90,360]{2,1,0:T(8,128)S(1)} %copy-done, f32[16,90,360]{2,1,0:T(8,128)S(1)} %copy-done.1, ...), custom_call_target="tpu_custom_call" | custom-call | tf_op jit(solution)/shard_map/stencil/pallas_call | solution.py:640
  216.3 4.7 %copy.31 = f32[2,16,90,360]{3,1,2,0:T(8,128)} copy(f32[2,16,90,360]{3,2,1,0:T(8,128)S(1)} %get-tuple-element.12) | data formatting | bytes 8294400 | tf_op jit(solution)/shard_map/stencil/pallas_call | solution.py:640
  221.0 2.6 %copy.32 = f32[16,90,360]{2,0,1:T(8,128)} copy(f32[16,90,360]{2,1,0:T(8,128)S(1)} %get-tuple-element.13) | data formatting | bytes 4147200 | tf_op jit(solution)/shard_map/stencil/pallas_call | solution.py:640
  223.6 2.6 %copy.33 = f32[16,90,360]{2,0,1:T(8,128)} copy(f32[16,90,360]{2,1,0:T(8,128)S(1)} %get-tuple-element.14) | data formatting | bytes 4147200 | tf_op jit(solution)/shard_map/stencil/pallas_call | solution.py:640
  (16 shorter events, 0.1 us)
Async XLA Ops:
  3.2 4.1 %copy-start.4 = (f32[16,90,360]{2,0,1:T(8,128)S(1)}, f32[16,90,360]{2,0,1:T(8,128)}, u32[]{:S(2)}) copy-start(f32[16,90,360]{2,0,1:T(8,128)} %param.17) | copy-start | bytes 6220804
  3.3 6.1 %slice-start.2 = ((s8[4423680]{0:T(1024)(128)(4,1)}), s8[4194304]{0:T(1024)(128)(4,1)S(1)}, s32[]{:S(2)}) async-start(s8[4423680]{0:T(1024)(128)(4,1)} %bitcast.6), calls=%async_computation.2 | async-start | bytes 8388608
  3.4 6.0 %slice-start.3 = ((s8[4423680]{0:T(1024)(128)(4,1)}), s8[229376]{0:T(1024)(128)(4,1)S(1)}, s32[]{:S(2)}) async-start(s8[4423680]{0:T(1024)(128)(4,1)} %bitcast.6), calls=%async_computation.3 | async-start | bytes 458752
  12.9 181.2 %slice-start = ((s8[4718592]{0:T(1024)(128)(4,1)}), s8[4194304]{0:T(1024)(128)(4,1)S(1)}, s32[]{:S(2)}) async-start(s8[4718592]{0:T(1024)(128)(4,1)} %bitcast.2), calls=%async_computation | async-start | bytes 8388608
  12.9 181.2 %slice-start.1 = ((s8[4718592]{0:T(1024)(128)(4,1)}), s8[524288]{0:T(1024)(128)(4,1)S(1)}, s32[]{:S(2)}) async-start(s8[4718592]{0:T(1024)(128)(4,1)} %bitcast.2), calls=%async_computation.1 | async-start | bytes 1048576
  194.1 1.7 copy-start
  195.8 1.7 copy-start.1
  197.5 0.9 copy-start.2
  198.4 0.9 copy-start.3

commit v2 on v0

v2 whole, which is shorter than its diff:
```python
import functools

import jax
import jax.numpy as jnp
import numpy as np
from jax import lax
from jax.experimental import pallas as pl
from jax.experimental.pallas import tpu as pltpu
from jax.sharding import PartitionSpec as P

NLON = 2880
NLAT = 1440
LEV = 16
ROWS = 90
COLS = 360
HALF = ROWS // 2
PC = 384
NP = 8
SUB = 8
NCH = 6
CR = ROWS // NCH
OFF1 = 0
OFF2 = 0
BLOCK = 9
MESH = pl.DeviceIdType.MESH
F32 = jnp.float32
BF16 = jnp.bfloat16


def split(table):
    hi = table.astype(np.float32).astype(BF16)
    lo = (table - hi.astype(np.float64)).astype(np.float32).astype(BF16)
    return np.asarray(hi), np.asarray(lo)


@functools.lru_cache(maxsize=None)
def value_tables():
    q = np.arange(PC)
    q = np.where(q == PC - 1, -1, q)
    forward = np.zeros((4, 2 * PC, PC))
    inverse = np.zeros((4, PC, 2 * PC))
    waves = np.full((4, PC), 1e9)
    m = np.arange(90)
    for g in range(4):
        parts = [(0, 0, 0), (4, 1, 0)] if g == 0 else [(g, 0, 1), (8 - g, 0, -1)]
        for slot, (r, half, sign) in enumerate(parts):
            k = 8 * m + r
            angle = 2.0 * np.pi * ((k[:, None] * q[None, :]) % NLON) / NLON
            cos, sin = np.cos(angle), np.sin(angle)
            re = slice(slot * 180, slot * 180 + 90)
            im = slice(slot * 180 + 90, slot * 180 + 180)
            waves[g, re] = k
            waves[g, im] = k
            weight = np.where(k == 0, 1.0, 2.0)[:, None] / NLON
            own = np.zeros((PC, 2 * PC))
            if sign == 0:
                own[re, half * PC : (half + 1) * PC] = cos
                own[im, half * PC : (half + 1) * PC] = -sin
            else:
                own[re, :PC] = cos
                own[im, :PC] = -sin
                own[re, PC:] = sign * sin
                own[im, PC:] = sign * cos
            scaled = own.copy()
            scaled[re] *= weight
            scaled[im] *= weight
            inverse[g] += scaled
            keep = np.concatenate([np.arange(PC) < COLS] * 2)
            forward[g] += (own * keep[None, :]).T
    used = np.concatenate([(np.arange(PC) <= COLS) | (np.arange(PC) == PC - 1)] * 2)
    inverse = inverse * used[None, None, :]
    return split(forward) + split(inverse) + (waves.astype(np.float32),)


@functools.lru_cache(maxsize=None)
def packed_tables():
    lane = np.arange(PC)
    wave = (lane + 1) // 2
    is_cos = (lane == 0) | (lane % 2 == 1)
    q = np.arange(PC)
    q = np.where(q == PC - 1, -1, q)
    used = (np.arange(PC) <= COLS) | (np.arange(PC) == PC - 1)
    forward = np.zeros((NP, 2, PC, PC))
    inverse = np.zeros((NP, 2, PC, PC))
    for p in range(NP):
        n = COLS * p + q
        angle = 2.0 * np.pi * ((wave[:, None] * n[None, :]) % NLON) / NLON
        base = np.where(is_cos[:, None], np.cos(angle), np.sin(angle))
        weight = np.where(wave == 0, 1.0, 2.0)[:, None] / NLON
        back = base * weight * used[None, :]
        ahead = (base * (np.arange(PC) < COLS)[None, :]).T
        forward[p, 0], forward[p, 1] = ahead, ahead[:, ::-1]
        inverse[p, 0], inverse[p, 1] = back, back[::-1]
    waves = np.stack([wave, wave[::-1]]).astype(np.float32)
    return split(forward) + split(inverse) + (waves,)


def dot3(x, hi, lo):
    x_hi = x.astype(BF16)
    x_lo = (x - x_hi.astype(F32)).astype(BF16)
    total = jnp.dot(x_hi, lo, preferred_element_type=F32)
    total += jnp.dot(x_lo, hi, preferred_element_type=F32)
    return total + jnp.dot(x_hi, hi, preferred_element_type=F32)


def wide(lim):
    return jnp.concatenate([lim, lim, lim], axis=-1)


def filter_kernel(
    w_ref, t_ref, h_ref, lim_ref, wv_ref, wp_ref,
    thi_ref, tlo_ref, uhi_ref, ulo_ref, fhi_ref, flo_ref, ghi_ref, glo_ref,
    state_ref,
    thi, tlo, uhi, ulo, fhi, flo, ghi, glo,
    recv, ret, strips, srecv, arecv, stage, obuf, xs, yb, zb, rawp, cols, side, zero,
    tab_sem, stage_sem, fsend, frecv, rsend, rrecv, ssend, srecv_sem, asend, arecv_sem,
    hsend, hrecv, lsend, lrecv, osem, zsem,
):
    lat = lax.axis_index("lat")
    lon = lax.axis_index("lon")
    north = lat < 8
    depth = jnp.where(north, lat, 15 - lat)
    partner = jnp.where(north, jnp.where(lat < 4, lat + 4, lat - 4), jnp.where(lat >= 12, lat - 4, lat + 4))
    is_packed = depth == 0
    is_value = (depth >= 1) & (depth <= 3)
    is_off = (depth == 5) | (depth == 6)
    served = jnp.where(is_off, partner, lat)
    served_depth = jnp.where(is_off, depth - 4, depth)
    n_off = jnp.where(served_depth == 1, OFF1, jnp.where(served_depth == 2, OFF2, 0))
    begin = jnp.where(served == 12, 2 * NCH // 3, 0)
    end = jnp.where(served == 3, NCH // 3, NCH)
    first = jnp.where(is_off, 0, jnp.maximum(begin, n_off))
    last = jnp.where(is_off, n_off, end)
    sources = (w_ref.at[0], w_ref.at[1], t_ref, h_ref)

    bar = pltpu.get_barrier_semaphore()
    for i in range(1, NP):
        pl.semaphore_signal(bar, inc=1, device_id=(lat, lax.rem(lon + i, NP)), device_id_type=MESH)
    for i in (1, 15):
        pl.semaphore_signal(bar, inc=1, device_id=(lax.rem(lat + i, 16), lon), device_id_type=MESH)
    n_signals = 9
    if OFF1 or OFF2:
        for i in range(NP):
            pl.semaphore_signal(bar, inc=1, device_id=(partner, lax.rem(lon + i, NP)), device_id_type=MESH)
        n_signals += NP

    tables = ((thi_ref, thi), (tlo_ref, tlo), (uhi_ref, uhi), (ulo_ref, ulo))
    packs = ((fhi_ref, fhi), (flo_ref, flo), (ghi_ref, ghi), (glo_ref, glo))

    @pl.when(is_packed)
    def _():
        for i, (src, dst) in enumerate(packs):
            pltpu.make_async_copy(src.at[lon], dst, tab_sem.at[i]).start()

    def part(g, rows):
        return sources[g // 2].at[rows, 8 * (g % 2) : 8 * (g % 2) + 8]

    def stage_copy(g, slot):
        return pltpu.make_async_copy(part(g, slice(0, ROWS)), stage.at[slot], stage_sem.at[slot])

    def state_part(p, start, count):
        return state_ref.at[p // 2, pl.ds(start, count), pl.ds(pl.multiple_of(lax.rem(p, 2) * 8, 8), 8)]

    @pl.when(is_packed | (depth >= 3))
    def _():
        stage_copy(0, 0).start()

    pl.semaphore_wait(bar, n_signals)

    @pl.when(is_value)
    def _():
        def per_copy(n, carry):
            c = begin + n // NP
            p = lax.rem(lon + n, NP)
            target = jnp.where(c < n_off, partner, lat)
            local = (c >= n_off) & (p == lon)
            dst = recv.at[c, lon]
            for g in range(NP):
                src = part(g, pl.ds(c * CR, CR))

                @pl.when((p == g) & jnp.logical_not(local))
                def _(src=src):
                    pltpu.make_async_remote_copy(
                        src_ref=src, dst_ref=dst, send_sem=fsend.at[c, p],
                        recv_sem=frecv.at[c, lon], device_id=(target, p), device_id_type=MESH,
                    ).start()

                @pl.when((p == g) & local)
                def _(src=src):
                    pltpu.make_async_copy(src, dst, frecv.at[c, lon]).start()

            return carry

        lax.fori_loop(0, (end - begin) * NP, per_copy, 0)

    @pl.when(is_value | is_off)
    def _():
        for i, (src, dst) in enumerate(tables):
            pltpu.make_async_copy(src, dst, tab_sem.at[i]).start()
        yb[...] = jnp.zeros_like(yb)

    def strip_copy(p):
        return pltpu.make_async_remote_copy(
            src_ref=strips.at[p], dst_ref=srecv.at[lon], send_sem=ssend.at[p],
            recv_sem=srecv_sem.at[lon], device_id=(lat, p), device_id_type=MESH,
        )

    @pl.when(is_packed)
    def _():
        xs[...] = jnp.zeros_like(xs)
        for i, (src, dst) in enumerate(packs):
            pltpu.make_async_copy(src.at[lon], dst, tab_sem.at[i]).wait()
        for g in range(NP):
            slot = g % 2
            if g + 1 < NP:
                stage_copy(g + 1, 1 - slot).start()
            stage_copy(g, slot).wait()
            xs[:, 0:COLS] = stage[slot].reshape(ROWS * SUB, COLS)
            low = dot3(xs[0 : HALF * SUB, :], fhi[0], flo[0]).reshape(HALF, SUB, PC)
            strips[g] = jnp.where(wp_ref[0:1, :] <= wide(lim_ref[0:HALF]), low, 0.0)
            high = dot3(xs[HALF * SUB :, :], fhi[1], flo[1]).reshape(HALF, SUB, PC)
            obuf[slot, 0:HALF] = jnp.where(wp_ref[1:2, :] <= wide(lim_ref[HALF:]), high, 0.0)

            def pair(i, carry, g=g, slot=slot):
                strips[g, i] += obuf[slot, HALF - 1 - i]
                return carry

            lax.fori_loop(0, HALF, pair, 0)

            @pl.when(lon != g)
            def _(g=g):
                strip_copy(g).start()

            @pl.when(lon == g)
            def _(g=g):
                pltpu.make_async_copy(strips.at[g], srecv.at[g], srecv_sem.at[g]).start()

        def wait_part(s, carry):
            pltpu.make_async_copy(srecv.at[s], srecv.at[s], srecv_sem.at[s]).wait()
            return carry

        lax.fori_loop(0, NP, wait_part, 0)

        def add(i, carry):
            total = srecv[0, i]
            for s in range(1, NP):
                total = total + srecv[s, i]
            arecv[lon, i] = total
            return carry

        lax.fori_loop(0, HALF, add, 0)

        def sum_to(p):
            return pltpu.make_async_remote_copy(
                src_ref=arecv.at[lon], dst_ref=arecv.at[lon], send_sem=asend.at[p],
                recv_sem=arecv_sem.at[lon], device_id=(lat, p), device_id_type=MESH,
            )

        def send(i, carry):
            sum_to(lax.rem(lon + i, NP)).start()
            return carry

        lax.fori_loop(1, NP, send, 0)

        def out_copy(p, slot):
            return pltpu.make_async_copy(obuf.at[slot], state_part(p, 1, ROWS), osem.at[slot])

        def back(i, carry):
            g = lax.rem(lon + i, NP)
            slot = lax.rem(i, 2)

            @pl.when(i > 0)
            def _():
                pltpu.make_async_copy(arecv.at[g], arecv.at[g], arecv_sem.at[g]).wait()

            @pl.when(i >= 2)
            def _():
                out_copy(g, slot).wait()

            spec = arecv[g]
            low = jnp.where(wp_ref[0:1, :] <= wide(lim_ref[0:HALF]), spec, 0.0).reshape(HALF * SUB, PC)
            obuf[slot, 0:HALF] = dot3(low, ghi[0], glo[0]).reshape(HALF, SUB, PC)

            def flip(j, carry):
                xs[pl.ds(pl.multiple_of(j * SUB, SUB), SUB), :] = arecv[g, HALF - 1 - j]
                return carry

            lax.fori_loop(0, HALF, flip, 0)
            high = xs[0 : HALF * SUB, :].reshape(HALF, SUB, PC)
            high = jnp.where(wp_ref[1:2, :] <= wide(lim_ref[HALF:]), high, 0.0).reshape(HALF * SUB, PC)
            obuf[slot, HALF:ROWS] = dot3(high, ghi[1], glo[1]).reshape(HALF, SUB, PC)
            out_copy(g, slot).start()
            return carry

        lax.fori_loop(0, NP, back, 0)
        for slot in range(2):
            out_copy(0, slot).wait()

        def sent(i, carry):
            p = lax.rem(lon + i, NP)
            sum_to(p).wait_send()
            strip_copy(p).wait_send()
            return carry

        lax.fori_loop(1, NP, sent, 0)

    @pl.when(is_value | is_off)
    def _():
        for i, (src, dst) in enumerate(tables):
            pltpu.make_async_copy(src, dst, tab_sem.at[i]).wait()

        half = np.float32(np.sqrt(0.5))

        def chunk(c, carry):
            def arrived(s, carry):
                pltpu.make_async_copy(recv.at[c, s], recv.at[c, s], frecv.at[c, s]).wait()
                return carry

            lax.fori_loop(0, NP, arrived, 0)

            def fold(r, carry):
                rows = pl.ds(pl.multiple_of(r * SUB, SUB), SUB)
                x = [recv[c, s, r] for s in range(NP)]
                s0, s1, s2, s3 = [x[j] + x[j + 4] for j in range(4)]
                d0, d1, d2, d3 = [x[j] - x[j + 4] for j in range(4)]
                plus, minus = half * (d1 + d3), half * (d1 - d3)
                out = (
                    (s0 + s2) + (s1 + s3), (s0 + s2) - (s1 + s3),
                    d0 + minus, -(d2 + plus),
                    s0 - s2, s3 - s1,
                    d0 - minus, d2 - plus,
                )
                for i in range(8):
                    yb[i, rows, 0:COLS] = out[i]
                return carry

            lax.fori_loop(0, CR, fold, 0)
            limit = wide(lim_ref[pl.ds(c * CR, CR)])

            def group(g, carry):
                spec = dot3(yb[2 * g], thi[g, 0:PC, :], tlo[g, 0:PC, :])
                spec += dot3(yb[2 * g + 1], thi[g, PC:, :], tlo[g, PC:, :])
                spec = jnp.where(wv_ref[g] <= limit, spec.reshape(CR, SUB, PC), 0.0).reshape(CR * SUB, PC)
                zb[2 * g] = dot3(spec, uhi[g, :, 0:PC], ulo[g, :, 0:PC])
                zb[2 * g + 1] = dot3(spec, uhi[g, :, PC:], ulo[g, :, PC:])
                return carry

            lax.fori_loop(0, 4, group, 0)

            def unfold(r, carry):
                rows = pl.ds(pl.multiple_of(r * SUB, SUB), SUB)
                a0, b0, a1, b1, a2, b2, a3, b3 = [zb[i, rows, :] for i in range(8)]
                even = (a0 + b0 + a2, a0 - b0 - b2, a0 + b0 - a2, a0 - b0 + b2)
                odd = (a1 + a3, half * ((a1 - a3) - (b1 + b3)), b3 - b1, half * ((a3 - a1) - (b1 + b3)))
                for j in range(4):
                    ret[c, j, r] = even[j] + odd[j]
                    ret[c, j + 4, r] = even[j] - odd[j]
                return carry

            lax.fori_loop(0, CR, unfold, 0)

            @pl.when(served_depth >= 2)
            def _():
                lane = lax.broadcasted_iota(jnp.int32, (SUB, 128), 1)

                def select(r, carry):
                    listed = wide(lim_ref[c * CR + r]) >= 0.0
                    for p in range(NP):
                        rawp[p, :, 0:COLS] = recv[c, p, r]
                    for p in range(NP):
                        east = recv[c, (p + 1) % NP, r, :, 0:1]
                        west = recv[c, (p + 7) % NP, r, :, COLS - 1 : COLS]
                        tail = jnp.where(lane == COLS - 256, east, rawp[p, :, 256:PC])
                        tail = jnp.where(lane == 127, west, tail)
                        raw = jnp.concatenate([rawp[p, :, 0:256], tail], axis=-1)
                        ret[c, p, r] = jnp.where(listed, ret[c, p, r], raw)
                    return carry

                lax.fori_loop(0, CR, select, 0)

            def give_back(i, carry):
                p = lax.rem(lon + i, NP)
                dst = state_part(lon, 1 + c * CR, CR)
                local = is_value & (p == lon)

                @pl.when(jnp.logical_not(local))
                def _():
                    pltpu.make_async_remote_copy(
                        src_ref=ret.at[c, p], dst_ref=dst, send_sem=rsend.at[c, p],
                        recv_sem=rrecv.at[c, lon], device_id=(served, p), device_id_type=MESH,
                    ).start()

                @pl.when(local)
                def _():
                    pltpu.make_async_copy(ret.at[c, p], dst, rrecv.at[c, lon]).start()

                return carry

            lax.fori_loop(0, NP, give_back, 0)
            return carry

        lax.fori_loop(first, last, chunk, 0)

        def returned(n, carry):
            c = first + n // NP
            p = lax.rem(n, NP)

            @pl.when(is_off | (p != lon))
            def _():
                pltpu.make_async_copy(ret.at[c, p], ret.at[c, p], rsend.at[c, p]).wait()

            return carry

        lax.fori_loop(0, (last - first) * NP, returned, 0)

    @pl.when(depth >= 3)
    def _():
        lane = lax.broadcasted_iota(jnp.int32, (SUB, 128), 1)
        for g in range(NP):
            slot = g % 2
            if g + 1 < NP:
                stage_copy(g + 1, 1 - slot).start()
            stage_copy(g, slot).wait()

            def gather(j, carry, slot=slot):
                head, tail = carry
                head = jnp.where(lane == j, stage[slot, j, :, 0:1], head)
                tail = jnp.where(lane == j, stage[slot, j, :, COLS - 1 : COLS], tail)
                return head, tail

            zeros = jnp.zeros((SUB, 128), F32)
            head, tail = lax.fori_loop(0, ROWS, gather, (zeros, zeros))
            cols[0, g] = head
            cols[1, g] = tail

        def side_copy(i):
            step = NP - 1 if i == 0 else 1
            return pltpu.make_async_remote_copy(
                src_ref=cols.at[i], dst_ref=side.at[i], send_sem=hsend.at[i], recv_sem=hrecv.at[i],
                device_id=(lat, lax.rem(lon + step, NP)), device_id_type=MESH,
            )

        for i in range(2):
            side_copy(i).start()
        stage_copy(0, 0).start()
        for i in range(2):
            side_copy(i).wait()

        own_start = jnp.where(lat == 3, ROWS // 3, 0)

        def out_copy(g, slot, act):
            full = pltpu.make_async_copy(obuf.at[slot], state_part(g, 1, ROWS), osem.at[slot])
            some = pltpu.make_async_copy(
                obuf.at[slot, pl.ds(own_start, 2 * ROWS // 3)],
                state_part(g, 1 + own_start, 2 * ROWS // 3), osem.at[slot],
            )

            @pl.when(depth > 3)
            def _():
                act(full)

            @pl.when(depth == 3)
            def _():
                act(some)

        for g in range(NP):
            slot = g % 2
            if g + 1 < NP:
                stage_copy(g + 1, 1 - slot).start()
            stage_copy(g, slot).wait()
            if g >= 2:
                out_copy(g, slot, lambda copy: copy.wait())
            obuf[slot, :, :, 0:COLS] = stage[slot]

            def insert(j, carry, g=g, slot=slot):
                east = jnp.sum(jnp.where(lane == j, side[0, g], 0.0), axis=1, keepdims=True)
                west = jnp.sum(jnp.where(lane == j, side[1, g], 0.0), axis=1, keepdims=True)
                tail = obuf[slot, j, :, 256:PC]
                tail = jnp.where(lane == COLS - 256, east, tail)
                obuf[slot, j, :, 256:PC] = jnp.where(lane == 127, west, tail)
                return carry

            lax.fori_loop(0, ROWS, insert, 0)
            out_copy(g, slot, lambda copy: copy.start())
        for slot in range(2):
            out_copy(0, slot, lambda copy: copy.wait())

    @pl.when(is_value)
    def _():
        def drain(n, carry):
            c = begin + n // NP
            p = lax.rem(n, NP)

            @pl.when((c < n_off) | (p != lon))
            def _():
                pltpu.make_async_copy(recv.at[c, p], recv.at[c, p], fsend.at[c, p]).wait()

            dst = state_part(p, 1 + c * CR, CR)
            pltpu.make_async_copy(dst, dst, rrecv.at[c, p]).wait()
            return carry

        lax.fori_loop(0, (end - begin) * NP, drain, 0)

    def edge_copy(i):
        row, there, step = ((1, ROWS + 1, 15), (ROWS, 0, 1))[i]
        return pltpu.make_async_remote_copy(
            src_ref=state_ref.at[:, row], dst_ref=state_ref.at[:, there],
            send_sem=lsend.at[i], recv_sem=lrecv.at[i],
            device_id=(lax.rem(lat + step, 16), lon), device_id_type=MESH,
        )

    def blank(row):
        return pltpu.make_async_copy(zero, state_ref.at[:, row], zsem)

    inner = (lat > 0, lat < 15)
    for i in range(2):
        @pl.when(inner[i])
        def _(i=i):
            edge_copy(i).start()

    for i, row in ((0, 0), (1, ROWS + 1)):
        @pl.when(jnp.logical_not(inner[i]))
        def _(row=row):
            zero[...] = jnp.zeros_like(zero)
            blank(row).start()
            blank(row).wait()

    for i in range(2):
        @pl.when(inner[i])
        def _(i=i):
            edge_copy(i).wait_send()

        @pl.when(inner[1 - i])
        def _(i=i):
            edge_copy(i).wait_recv()


def stencil_kernel(trig_ref, state_ref, wind_out, t_out, h_out):
    base = lax.axis_index("lat") * ROWS + pl.program_id(0) * BLOCK

    def dx(a):
        return pltpu.roll(a, PC - 1, 1) - pltpu.roll(a, 1, 1)

    def one(r, carry):
        at = base + r
        cos_n, cos_s = trig_ref[0, at], trig_ref[0, at + 2]
        inv = trig_ref[1, at + 1]
        turn = 0.3 * trig_ref[2, at + 1]
        u, v, t, h = [state_ref[k, r + 1] for k in range(4)]
        un, vn, tn, hn = [state_ref[k, r] for k in range(4)]
        us, vs, ts, hs = [state_ref[k, r + 2] for k in range(4)]
        cu = (0.025 * inv) * u
        cv = 0.1 * v
        new_h = h - (0.025 * inv) * dx(u * h) - (0.1 * inv) * (vs * hs * cos_s - vn * hn * cos_n)
        new_t = t - cu * dx(t) - cv * (ts - tn)
        new_u = u - cu * dx(u) - cv * (us - un) - (0.05 * inv) * dx(h) + turn * v
        new_v = v - cu * dx(v) - cv * (vs - vn) - 0.15 * (hs - hn) - turn * u
        wind_out[0, r] = new_u[:, 0:COLS]
        wind_out[1, r] = new_v[:, 0:COLS]
        t_out[r] = new_t[:, 0:COLS]
        h_out[r] = new_h[:, 0:COLS]
        return carry

    lax.fori_loop(0, BLOCK, one, 0, unroll=True)


@functools.lru_cache(maxsize=None)
def trig_table():
    row = np.arange(-1, NLAT + 1).astype(np.float32) + np.float32(0.5)
    angle = (row * np.float32(np.pi / NLAT)).astype(np.float64)
    cos = np.sin(angle).astype(np.float32)
    sin = -np.cos(angle).astype(np.float32)
    return np.stack([cos, (1.0 / cos.astype(np.float64)).astype(np.float32), sin])


def body(winds, theta, thick, polar_rows, cutoffs):
    lat = lax.axis_index("lat")
    served = jnp.where((lat >= 4) & (lat < 8), lat - 4, jnp.where((lat >= 8) & (lat < 12), lat + 4, lat))
    rows = served * ROWS + jnp.arange(ROWS, dtype=jnp.int32)
    hits = polar_rows[None, :] == rows[:, None]
    limit = jnp.max(jnp.where(hits, cutoffs[None, :], -1), axis=1).astype(F32)
    lim = jnp.broadcast_to(limit[:, None, None], (ROWS, SUB, 128))
    thi, tlo, uhi, ulo, wv = value_tables()
    fhi, flo, ghi, glo, wp = packed_tables()
    vm = pl.BlockSpec(memory_space=pltpu.VMEM)
    hbm = pl.BlockSpec(memory_space=pl.ANY)
    dma = pltpu.SemaphoreType.DMA
    state = pl.pallas_call(
        filter_kernel,
        out_shape=jax.ShapeDtypeStruct((4, ROWS + 2, LEV, PC), F32),
        in_specs=[hbm, hbm, hbm, vm, vm, vm] + [hbm] * 8,
        out_specs=hbm,
        scratch_shapes=[
            pltpu.VMEM((4, 2 * PC, PC), BF16), pltpu.VMEM((4, 2 * PC, PC), BF16),
            pltpu.VMEM((4, PC, 2 * PC), BF16), pltpu.VMEM((4, PC, 2 * PC), BF16),
            pltpu.VMEM((2, PC, PC), BF16), pltpu.VMEM((2, PC, PC), BF16),
            pltpu.VMEM((2, PC, PC), BF16), pltpu.VMEM((2, PC, PC), BF16),
            pltpu.VMEM((NCH, NP, CR, SUB, COLS), F32),
            pltpu.VMEM((NCH, NP, CR, SUB, PC), F32),
            pltpu.VMEM((NP, HALF, SUB, PC), F32),
            pltpu.VMEM((NP, HALF, SUB, PC), F32),
            pltpu.VMEM((NP, HALF, SUB, PC), F32),
            pltpu.VMEM((2, ROWS, SUB, COLS), F32),
            pltpu.VMEM((2, ROWS, SUB, PC), F32),
            pltpu.VMEM((ROWS * SUB, PC), F32),
            pltpu.VMEM((8, CR * SUB, PC), F32),
            pltpu.VMEM((8, CR * SUB, PC), F32),
            pltpu.VMEM((NP, SUB, PC), F32),
            pltpu.VMEM((2, NP, SUB, 128), F32),
            pltpu.VMEM((2, NP, SUB, 128), F32),
            pltpu.VMEM((4, LEV, PC), F32),
            dma((4,)), dma((2,)),
            dma((NCH, NP)), dma((NCH, NP)), dma((NCH, NP)), dma((NCH, NP)),
            dma((NP,)), dma((NP,)), dma((NP,)), dma((NP,)),
            dma((2,)), dma((2,)), dma((2,)), dma((2,)), dma((2,)), dma,
        ],
        compiler_params=pltpu.CompilerParams(
            collective_id=1, has_side_effects=True, vmem_limit_bytes=58 * 2**20
        ),
        name="polar_filter",
    )(
        winds.transpose(0, 2, 1, 3), theta.transpose(1, 0, 2), thick.transpose(1, 0, 2), lim,
        jnp.asarray(wv)[:, None, :], jnp.asarray(wp), thi, tlo, uhi, ulo, fhi, flo, ghi, glo,
    )
    new_winds, new_t, new_h = pl.pallas_call(
        stencil_kernel,
        grid=(ROWS // BLOCK,),
        out_shape=(
            jax.ShapeDtypeStruct((2, ROWS, LEV, COLS), F32),
            jax.ShapeDtypeStruct((ROWS, LEV, COLS), F32),
            jax.ShapeDtypeStruct((ROWS, LEV, COLS), F32),
        ),
        in_specs=[
            pl.BlockSpec(memory_space=pltpu.SMEM),
            pl.BlockSpec(
                (pl.Element(4), pl.Element(BLOCK + 2), pl.Element(LEV), pl.Element(PC)),
                lambda i: (0, i * BLOCK, 0, 0),
            ),
        ],
        out_specs=(
            pl.BlockSpec((2, BLOCK, LEV, COLS), lambda i: (0, i, 0, 0)),
            pl.BlockSpec((BLOCK, LEV, COLS), lambda i: (i, 0, 0)),
            pl.BlockSpec((BLOCK, LEV, COLS), lambda i: (i, 0, 0)),
        ),
        compiler_params=pltpu.CompilerParams(vmem_limit_bytes=32 * 2**20),
        name="stencil",
    )(jnp.asarray(trig_table()), state)
    return new_winds.transpose(0, 2, 1, 3), new_t.transpose(1, 0, 2), new_h.transpose(1, 0, 2)


def solution(mesh):
    in_specs = (P(None, None, "lat", "lon"), P(None, "lat", "lon"), P(None, "lat", "lon"), P(), P())
    out_specs = (P(None, None, "lat", "lon"), P(None, "lat", "lon"), P(None, "lat", "lon"))
    return jax.shard_map(body, mesh=mesh, in_specs=in_specs, out_specs=out_specs, check_vma=False)
```

time: 481 us -> 211 us (0.44)
  the two profiles are of different devices: /device:TPU:97 before, /device:TPU:71 now
where the time goes in v2:
time: 211 us
  Pallas kernels  205 us (97%)
  local copies, waits for them, and re-layouts  4.47 us (2%)
    pallas_call x1, Pallas kernels, body(): pl.pallas_call(filter_kernel, out_shape=jax.ShapeDtypeStruct((4, ROWS + 2...  195 us
    pallas_call x1, Pallas kernels, body(): pl.pallas_call(stencil_kernel, grid=(ROWS // BLOCK,), out_shape=(jax.Shap...  9.7 us

profile of v2, /device:TPU:71, one launch (start us, length us, event | category | flops | bytes accessed | tf_op | source)
XLA Modules:
  0.0 210.9 jit_solution(16153060414547094453)
XLA Ops:
  0.7 0.9 select_reduce_fusion
  1.6 0.9 broadcast_in_dim.26.lim_ref
  2.5 0.0 copy-start.1
  2.5 195.1 %polar_filter.1.state_ref = f32[4,92,16,384]{3,2,1,0:T(8,128)} custom-call(f32[2,90,16,360]{3,2,1,0:T(8,128)} %bitcast.6, f32[90,16,360]{2,1,0:T(8,128)} %bitcast.7, f32[90,16,360]{2,1,0:T(8,128)} %bitcast.8, f32[90,8,128]{2,1,0:T(8,128)} %broadcast_in_dim.26.lim_ref, f32[4,1,384]{2,1,0:T(1,128)} %constant.56.wv_ref, f32[2,384]{1,0:T(2,128)} %constant.43.clone.wp_ref, ...), custom_call_target="tpu_custom_call" | custom-call | tf_op jit(solution)/shard_map/polar_filter/pallas_call | solution.py:588
  197.6 0.0 copy-done.1
  197.6 0.0 copy-start
  197.6 3.6 %copy-done = f32[4,92,16,384]{3,2,1,0:T(8,128)S(1)} copy-done((f32[4,92,16,384]{3,2,1,0:T(8,128)S(1)}, f32[4,92,16,384]{3,2,1,0:T(8,128)}, u32[]{:S(2)}) %copy-start) | copy-done | bytes 9043992
  201.2 9.7 %stencil.1 = (f32[2,90,16,360]{3,2,1,0:T(8,128)}, f32[90,16,360]{2,1,0:T(8,128)}, f32[90,16,360]{2,1,0:T(8,128)}) custom-call(f32[3,1442]{1,0:T(4,128)S(1)} %copy-done.1, f32[4,92,16,384]{3,2,1,0:T(8,128)S(1)} %copy-done), custom_call_target="tpu_custom_call" | custom-call | tf_op jit(solution)/shard_map/stencil/pallas_call | solution.py:625
  (2 shorter events, 0.0 us)
Async XLA Ops:
  2.5 195.1 %copy-start.1 = (f32[3,1442]{1,0:T(4,128)S(1)}, f32[3,1442]{1,0:T(4,128)}, u32[]{:S(2)}) copy-start(f32[3,1442]{1,0:T(4,128)} %constant.52.clone.trig_ref) | copy-start | bytes 51916
  197.6 3.6 %copy-start = (f32[4,92,16,384]{3,2,1,0:T(8,128)S(1)}, f32[4,92,16,384]{3,2,1,0:T(8,128)}, u32[]{:S(2)}) copy-start(f32[4,92,16,384]{3,2,1,0:T(8,128)} %polar_filter.1.state_ref) | copy-start | bytes 27131908

commit v3 on v2

--- a/solution.py
+++ b/solution.py
@@ -17,10 +17,11 @@
 PC = 384
 NP = 8
 SUB = 8
-NCH = 6
+NCH = 9
 CR = ROWS // NCH
-OFF1 = 0
-OFF2 = 0
+OFF1 = 6
+OFF2 = 5
+MID = 5
 BLOCK = 9
 MESH = pl.DeviceIdType.MESH
 F32 = jnp.float32
@@ -112,9 +113,9 @@
     thi_ref, tlo_ref, uhi_ref, ulo_ref, fhi_ref, flo_ref, ghi_ref, glo_ref,
     state_ref,
     thi, tlo, uhi, ulo, fhi, flo, ghi, glo,
-    recv, ret, strips, srecv, arecv, stage, obuf, xs, yb, zb, rawp, cols, side, zero,
+    recv, ret, strips, srecv, arecv, stage, obuf, xs, yb, zb, rawp, cols, side, zero, home,
     tab_sem, stage_sem, fsend, frecv, rsend, rrecv, ssend, srecv_sem, asend, arecv_sem,
-    hsend, hrecv, lsend, lrecv, osem, zsem,
+    hsend, hrecv, lsend, lrecv, osem, zsem, xsend, xrecv,
 ):
     lat = lax.axis_index("lat")
     lon = lax.axis_index("lon")
@@ -161,37 +162,57 @@
     def state_part(p, start, count):
         return state_ref.at[p // 2, pl.ds(start, count), pl.ds(pl.multiple_of(lax.rem(p, 2) * 8, 8), 8)]
 
-    @pl.when(is_packed | (depth >= 3))
+    @pl.when(depth >= 3)
     def _():
         stage_copy(0, 0).start()
 
     pl.semaphore_wait(bar, n_signals)
 
+    def relay(c, k):
+        return pltpu.make_async_remote_copy(
+            src_ref=sources[k].at[pl.ds(c * CR, CR)], dst_ref=home.at[c, k],
+            send_sem=xsend.at[c, k], recv_sem=xrecv.at[c, k],
+            device_id=(partner, lon), device_id_type=MESH,
+        )
+
+    def relay_all(c, act):
+        for k in range(4):
+            act(relay(c, k))
+
+    def relay_next(c, carry):
+        relay_all(c - 2, lambda copy: copy.wait_send())
+        relay_all(c, lambda copy: copy.start())
+        return carry
+
+    def relay_only(c, carry):
+        relay_all(c, lambda copy: copy.start())
+        return carry
+
     @pl.when(is_value)
     def _():
+        lax.fori_loop(0, jnp.minimum(n_off, 2), relay_only, 0)
+
         def per_copy(n, carry):
-            c = begin + n // NP
+            c = first + n // NP
             p = lax.rem(lon + n, NP)
-            target = jnp.where(c < n_off, partner, lat)
-            local = (c >= n_off) & (p == lon)
             dst = recv.at[c, lon]
             for g in range(NP):
                 src = part(g, pl.ds(c * CR, CR))
 
-                @pl.when((p == g) & jnp.logical_not(local))
+                @pl.when((p == g) & (p != lon))
                 def _(src=src):
                     pltpu.make_async_remote_copy(
                         src_ref=src, dst_ref=dst, send_sem=fsend.at[c, p],
-                        recv_sem=frecv.at[c, lon], device_id=(target, p), device_id_type=MESH,
+                        recv_sem=frecv.at[c, lon], device_id=(lat, p), device_id_type=MESH,
                     ).start()
 
-                @pl.when((p == g) & local)
+                @pl.when((p == g) & (p == lon))
                 def _(src=src):
                     pltpu.make_async_copy(src, dst, frecv.at[c, lon]).start()
 
             return carry
 
-        lax.fori_loop(0, (end - begin) * NP, per_copy, 0)
+        lax.fori_loop(0, (last - first) * NP, per_copy, 0)
 
     @pl.when(is_value | is_off)
     def _():
@@ -210,99 +231,189 @@
         xs[...] = jnp.zeros_like(xs)
         for i, (src, dst) in enumerate(packs):
             pltpu.make_async_copy(src.at[lon], dst, tab_sem.at[i]).wait()
+
+        def load_part(g, slot):
+            half = pl.ds(pl.multiple_of(lax.rem(g, 2) * 8, 8), 8)
+            for k in range(4):
+                @pl.when(g // 2 == k)
+                def _(k=k):
+                    pltpu.make_async_copy(sources[k].at[:, half], stage.at[slot], stage_sem.at[slot]).start()
+
+        load_part(lax.rem(lon + 1, NP), 0)
+
+        def ahead(i, carry):
+            g = lax.rem(lon + 1 + i, NP)
+            slot = lax.rem(i, 2)
+
+            @pl.when(i + 1 < NP)
+            def _():
+                load_part(lax.rem(g + 1, NP), 1 - slot)
+
+            pltpu.make_async_copy(stage.at[slot], stage.at[slot], stage_sem.at[slot]).wait()
+            xs[:, 0:COLS] = stage[slot].reshape(ROWS * SUB, COLS)
+            low = dot3(xs[0 : HALF * SUB, :], fhi[0], flo[0]).reshape(HALF, SUB, PC)
+            strips[g] = jnp.where(wp_ref[0:1, :] <= wide(lim_ref[0:HALF]), low, 0.0)
+            high = dot3(xs[HALF * SUB :, :], fhi[1], flo[1]).reshape(HALF, SUB, PC)
+            obuf[slot, 0:HALF] = jnp.where(wp_ref[1:2, :] <= wide(lim_ref[HALF:]), high, 0.0)
+
+            def pair(j, carry):
+                strips[g, j] += obuf[slot, HALF - 1 - j]
+                return carry
+
+            lax.fori_loop(0, HALF, pair, 0, unroll=9)
+
+            @pl.when(lon != g)
+            def _():
+                strip_copy(g).start()
+
+            @pl.when(lon == g)
+            def _():
+                pltpu.make_async_copy(strips.at[g], srecv.at[g], srecv_sem.at[g]).start()
+
+            return carry
+
+        lax.fori_loop(0, NP, ahead, 0)
+
+        def wait_part(s, carry):
+            pltpu.make_async_copy(srecv.at[s], srecv.at[s], srecv_sem.at[s]).wait()
+            return carry
+
+        lax.fori_loop(0, NP, wait_part, 0)
+
+        def add(i, carry):
+            total = srecv[0, i]
+            for s in range(1, NP):
+                total = total + srecv[s, i]
+            arecv[lon, i] = total
+            return carry
+
+        lax.fori_loop(0, HALF, add, 0, unroll=5)
+
+        def sum_to(p):
+            return pltpu.make_async_remote_copy(
+                src_ref=arecv.at[lon], dst_ref=arecv.at[lon], send_sem=asend.at[p],
+                recv_sem=arecv_sem.at[lon], device_id=(lat, p), device_id_type=MESH,
+            )
+
+        def send(i, carry):
+            sum_to(lax.rem(lon + i, NP)).start()
+            return carry
+
+        lax.fori_loop(1, NP, send, 0)
+
+        def out_copy(p, slot):
+            return pltpu.make_async_copy(obuf.at[slot], state_part(p, 1, ROWS), osem.at[slot])
+
+        def back(i, carry):
+            g = lax.rem(lon + i, NP)
+            slot = lax.rem(i, 2)
+
+            @pl.when(i > 0)
+            def _():
+                pltpu.make_async_copy(arecv.at[g], arecv.at[g], arecv_sem.at[g]).wait()
+
+            @pl.when(i >= 2)
+            def _():
+                out_copy(g, slot).wait()
+
+            spec = arecv[g]
+            low = jnp.where(wp_ref[0:1, :] <= wide(lim_ref[0:HALF]), spec, 0.0).reshape(HALF * SUB, PC)
+            obuf[slot, 0:HALF] = dot3(low, ghi[0], glo[0]).reshape(HALF, SUB, PC)
+
+            def flip(j, carry):
+                xs[pl.ds(pl.multiple_of(j * SUB, SUB), SUB), :] = arecv[g, HALF - 1 - j]
+                return carry
+
+            lax.fori_loop(0, HALF, flip, 0, unroll=9)
+            high = xs[0 : HALF * SUB, :].reshape(HALF, SUB, PC)
+            high = jnp.where(wp_ref[1:2, :] <= wide(lim_ref[HALF:]), high, 0.0).reshape(HALF * SUB, PC)
+            obuf[slot, HALF:ROWS] = dot3(high, ghi[1], glo[1]).reshape(HALF, SUB, PC)
+            out_copy(g, slot).start()
+            return carry
+
+        lax.fori_loop(0, NP, back, 0)
+        for slot in range(2):
+            out_copy(0, slot).wait()
+
+        def sent(i, carry):
+            p = lax.rem(lon + i, NP)
+            sum_to(p).wait_send()
+            strip_copy(p).wait_send()
+            return carry
+
+        lax.fori_loop(1, NP, sent, 0)
+
+    @pl.when(depth >= 3)
+    def _():
+        lane = lax.broadcasted_iota(jnp.int32, (SUB, 128), 1)
         for g in range(NP):
             slot = g % 2
             if g + 1 < NP:
                 stage_copy(g + 1, 1 - slot).start()
             stage_copy(g, slot).wait()
-            xs[:, 0:COLS] = stage[slot].reshape(ROWS * SUB, COLS)
-            low = dot3(xs[0 : HALF * SUB, :], fhi[0], flo[0]).reshape(HALF, SUB, PC)
-            strips[g] = jnp.where(wp_ref[0:1, :] <= wide(lim_ref[0:HALF]), low, 0.0)
-            high = dot3(xs[HALF * SUB :, :], fhi[1], flo[1]).reshape(HALF, SUB, PC)
-            obuf[slot, 0:HALF] = jnp.where(wp_ref[1:2, :] <= wide(lim_ref[HALF:]), high, 0.0)
-
-            def pair(i, carry, g=g, slot=slot):
-                strips[g, i] += obuf[slot, HALF - 1 - i]
-                return carry
-
-            lax.fori_loop(0, HALF, pair, 0)
-
-            @pl.when(lon != g)
-            def _(g=g):
-                strip_copy(g).start()
-
-            @pl.when(lon == g)
-            def _(g=g):
-                pltpu.make_async_copy(strips.at[g], srecv.at[g], srecv_sem.at[g]).start()
-
-        def wait_part(s, carry):
-            pltpu.make_async_copy(srecv.at[s], srecv.at[s], srecv_sem.at[s]).wait()
-            return carry
-
-        lax.fori_loop(0, NP, wait_part, 0)
-
-        def add(i, carry):
-            total = srecv[0, i]
-            for s in range(1, NP):
-                total = total + srecv[s, i]
-            arecv[lon, i] = total
-            return carry
-
-        lax.fori_loop(0, HALF, add, 0)
-
-        def sum_to(p):
+
+            def gather(j, carry, slot=slot):
+                head, tail = carry
+                head = jnp.where(lane == j, stage[slot, j, :, 0:1], head)
+                tail = jnp.where(lane == j, stage[slot, j, :, COLS - 1 : COLS], tail)
+                return head, tail
+
+            zeros = jnp.zeros((SUB, 128), F32)
+            head, tail = lax.fori_loop(0, ROWS, gather, (zeros, zeros), unroll=18)
+            cols[0, g] = head
+            cols[1, g] = tail
+
+        def side_copy(i):
+            step = NP - 1 if i == 0 else 1
             return pltpu.make_async_remote_copy(
-                src_ref=arecv.at[lon], dst_ref=arecv.at[lon], send_sem=asend.at[p],
-                recv_sem=arecv_sem.at[lon], device_id=(lat, p), device_id_type=MESH,
+                src_ref=cols.at[i], dst_ref=side.at[i], send_sem=hsend.at[i], recv_sem=hrecv.at[i],
+                device_id=(lat, lax.rem(lon + step, NP)), device_id_type=MESH,
             )
 
-        def send(i, carry):
-            sum_to(lax.rem(lon + i, NP)).start()
-            return carry
-
-        lax.fori_loop(1, NP, send, 0)
-
-        def out_copy(p, slot):
-            return pltpu.make_async_copy(obuf.at[slot], state_part(p, 1, ROWS), osem.at[slot])
-
-        def back(i, carry):
-            g = lax.rem(lon + i, NP)
-            slot = lax.rem(i, 2)
-
-            @pl.when(i > 0)
-            def _():
-                pltpu.make_async_copy(arecv.at[g], arecv.at[g], arecv_sem.at[g]).wait()
-
-            @pl.when(i >= 2)
-            def _():
-                out_copy(g, slot).wait()
-
-            spec = arecv[g]
-            low = jnp.where(wp_ref[0:1, :] <= wide(lim_ref[0:HALF]), spec, 0.0).reshape(HALF * SUB, PC)
-            obuf[slot, 0:HALF] = dot3(low, ghi[0], glo[0]).reshape(HALF, SUB, PC)
-
-            def flip(j, carry):
-                xs[pl.ds(pl.multiple_of(j * SUB, SUB), SUB), :] = arecv[g, HALF - 1 - j]
-                return carry
-
-            lax.fori_loop(0, HALF, flip, 0)
-            high = xs[0 : HALF * SUB, :].reshape(HALF, SUB, PC)
-            high = jnp.where(wp_ref[1:2, :] <= wide(lim_ref[HALF:]), high, 0.0).reshape(HALF * SUB, PC)
-            obuf[slot, HALF:ROWS] = dot3(high, ghi[1], glo[1]).reshape(HALF, SUB, PC)
-            out_copy(g, slot).start()
-            return carry
-
-        lax.fori_loop(0, NP, back, 0)
+        for i in range(2):
+            side_copy(i).start()
+        stage_copy(0, 0).start()
+        for i in range(2):
+            side_copy(i).wait()
+
+        own_start = jnp.where(lat == 3, ROWS // 3, 0)
+
+        def out_copy(g, slot, act):
+            full = pltpu.make_async_copy(obuf.at[slot], state_part(g, 1, ROWS), osem.at[slot])
+            some = pltpu.make_async_copy(
+                obuf.at[slot, pl.ds(own_start, 2 * ROWS // 3)],
+                state_part(g, 1 + own_start, 2 * ROWS // 3), osem.at[slot],
+            )
+
+            @pl.when(depth > 3)
+            def _():
+                act(full)
+
+            @pl.when(depth == 3)
+            def _():
+                act(some)
+
+        for g in range(NP):
+            slot = g % 2
+            if g + 1 < NP:
+                stage_copy(g + 1, 1 - slot).start()
+            stage_copy(g, slot).wait()
+            if g >= 2:
+                out_copy(g, slot, lambda copy: copy.wait())
+
+            def insert(j, carry, g=g, slot=slot):
+                obuf[slot, j, :, 0:COLS] = stage[slot, j]
+                east = pltpu.roll(side[0, g], lax.rem(COLS - 256 + 128 - j, 128), 1)
+                west = pltpu.roll(side[1, g], 127 - j, 1)
+                tail = obuf[slot, j, :, 256:PC]
+                tail = jnp.where(lane == COLS - 256, east, tail)
+                obuf[slot, j, :, 256:PC] = jnp.where(lane == 127, west, tail)
+                return carry
+
+            lax.fori_loop(0, ROWS, insert, 0, unroll=9)
+            out_copy(g, slot, lambda copy: copy.start())
         for slot in range(2):
-            out_copy(0, slot).wait()
-
-        def sent(i, carry):
-            p = lax.rem(lon + i, NP)
-            sum_to(p).wait_send()
-            strip_copy(p).wait_send()
-            return carry
-
-        lax.fori_loop(1, NP, sent, 0)
+            out_copy(0, slot, lambda copy: copy.wait())
 
     @pl.when(is_value | is_off)
     def _():
@@ -399,7 +510,44 @@
             lax.fori_loop(0, NP, give_back, 0)
             return carry
 
-        lax.fori_loop(first, last, chunk, 0)
+        def pass_on(c):
+            relay_all(c, lambda copy: copy.wait_recv())
+            dst = recv.at[c, lon]
+
+            def home_part(p):
+                return home.at[c, p // 2, :, pl.ds(pl.multiple_of(lax.rem(p, 2) * 8, 8), 8)]
+
+            def to_owner(i, carry):
+                p = lax.rem(lon + i, NP)
+                pltpu.make_async_remote_copy(
+                    src_ref=home_part(p), dst_ref=dst, send_sem=fsend.at[c, p],
+                    recv_sem=frecv.at[c, lon], device_id=(lat, p), device_id_type=MESH,
+                ).start()
+                return carry
+
+            lax.fori_loop(1, NP, to_owner, 0)
+            pltpu.make_async_copy(home_part(lon), dst, frecv.at[c, lon]).start()
+
+        def step(n, carry):
+            @pl.when(is_off & (n < last))
+            def _():
+                pass_on(n)
+
+            @pl.when(n > first)
+            def _():
+                chunk(n - 1, 0)
+
+            return carry
+
+        @pl.when(is_value)
+        def _():
+            lax.fori_loop(2, jnp.minimum(n_off, MID), relay_next, 0)
+
+        lax.fori_loop(first, last + 1, step, 0)
+
+        @pl.when(is_value)
+        def _():
+            lax.fori_loop(MID, n_off, relay_next, 0)
 
         def returned(n, carry):
             c = first + n // NP
@@ -409,81 +557,13 @@
             def _():
                 pltpu.make_async_copy(ret.at[c, p], ret.at[c, p], rsend.at[c, p]).wait()
 
+            @pl.when(p != lon)
+            def _():
+                pltpu.make_async_copy(recv.at[c, p], recv.at[c, p], fsend.at[c, p]).wait()
+
             return carry
 
         lax.fori_loop(0, (last - first) * NP, returned, 0)
-
-    @pl.when(depth >= 3)
-    def _():
-        lane = lax.broadcasted_iota(jnp.int32, (SUB, 128), 1)
-        for g in range(NP):
-            slot = g % 2
-            if g + 1 < NP:
-                stage_copy(g + 1, 1 - slot).start()
-            stage_copy(g, slot).wait()
-
-            def gather(j, carry, slot=slot):
-                head, tail = carry
-                head = jnp.where(lane == j, stage[slot, j, :, 0:1], head)
-                tail = jnp.where(lane == j, stage[slot, j, :, COLS - 1 : COLS], tail)
-                return head, tail
-
-            zeros = jnp.zeros((SUB, 128), F32)
-            head, tail = lax.fori_loop(0, ROWS, gather, (zeros, zeros))
-            cols[0, g] = head
-            cols[1, g] = tail
-
-        def side_copy(i):
-            step = NP - 1 if i == 0 else 1
-            return pltpu.make_async_remote_copy(
-                src_ref=cols.at[i], dst_ref=side.at[i], send_sem=hsend.at[i], recv_sem=hrecv.at[i],
-                device_id=(lat, lax.rem(lon + step, NP)), device_id_type=MESH,
-            )
-
-        for i in range(2):
-            side_copy(i).start()
-        stage_copy(0, 0).start()
-        for i in range(2):
-            side_copy(i).wait()
-
-        own_start = jnp.where(lat == 3, ROWS // 3, 0)
-
-        def out_copy(g, slot, act):
-            full = pltpu.make_async_copy(obuf.at[slot], state_part(g, 1, ROWS), osem.at[slot])
-            some = pltpu.make_async_copy(
-                obuf.at[slot, pl.ds(own_start, 2 * ROWS // 3)],
-                state_part(g, 1 + own_start, 2 * ROWS // 3), osem.at[slot],
-            )
-
-            @pl.when(depth > 3)
-            def _():
-                act(full)
-
-            @pl.when(depth == 3)
-            def _():
-                act(some)
-
-        for g in range(NP):
-            slot = g % 2
-            if g + 1 < NP:
-                stage_copy(g + 1, 1 - slot).start()
-            stage_copy(g, slot).wait()
-            if g >= 2:
-                out_copy(g, slot, lambda copy: copy.wait())
-            obuf[slot, :, :, 0:COLS] = stage[slot]
-
-            def insert(j, carry, g=g, slot=slot):
-                east = jnp.sum(jnp.where(lane == j, side[0, g], 0.0), axis=1, keepdims=True)
-                west = jnp.sum(jnp.where(lane == j, side[1, g], 0.0), axis=1, keepdims=True)
-                tail = obuf[slot, j, :, 256:PC]
-                tail = jnp.where(lane == COLS - 256, east, tail)
-                obuf[slot, j, :, 256:PC] = jnp.where(lane == 127, west, tail)
-                return carry
-
-            lax.fori_loop(0, ROWS, insert, 0)
-            out_copy(g, slot, lambda copy: copy.start())
-        for slot in range(2):
-            out_copy(0, slot, lambda copy: copy.wait())
 
     @pl.when(is_value)
     def _():
@@ -491,15 +571,17 @@
             c = begin + n // NP
             p = lax.rem(n, NP)
 
-            @pl.when((c < n_off) | (p != lon))
-            def _():
-                pltpu.make_async_copy(recv.at[c, p], recv.at[c, p], fsend.at[c, p]).wait()
-
             dst = state_part(p, 1 + c * CR, CR)
             pltpu.make_async_copy(dst, dst, rrecv.at[c, p]).wait()
             return carry
 
         lax.fori_loop(0, (end - begin) * NP, drain, 0)
+
+        def relayed(c, carry):
+            relay_all(c, lambda copy: copy.wait_send())
+            return carry
+
+        lax.fori_loop(jnp.maximum(n_off - 2, 0), n_off, relayed, 0)
 
     def edge_copy(i):
         row, there, step = ((1, ROWS + 1, 15), (ROWS, 0, 1))[i]
@@ -609,13 +691,15 @@
             pltpu.VMEM((2, NP, SUB, 128), F32),
             pltpu.VMEM((2, NP, SUB, 128), F32),
             pltpu.VMEM((4, LEV, PC), F32),
+            pltpu.VMEM((max(OFF1, OFF2), 4, CR, LEV, COLS), F32),
             dma((4,)), dma((2,)),
             dma((NCH, NP)), dma((NCH, NP)), dma((NCH, NP)), dma((NCH, NP)),
             dma((NP,)), dma((NP,)), dma((NP,)), dma((NP,)),
             dma((2,)), dma((2,)), dma((2,)), dma((2,)), dma((2,)), dma,
+            dma((NCH, 4)), dma((NCH, 4)),
         ],
         compiler_params=pltpu.CompilerParams(
-            collective_id=1, has_side_effects=True, vmem_limit_bytes=58 * 2**20
+            collective_id=1, has_side_effects=True, vmem_limit_bytes=60 * 2**20
         ),
         name="polar_filter",
     )(

time: 211 us -> 140 us (0.66)
  the two profiles are of different devices: /device:TPU:71 before, /device:TPU:97 now
where the time goes in v3:
time: 140 us
  Pallas kernels  134 us (96%)
  local copies, waits for them, and re-layouts  4.47 us (3%)
    pallas_call x1, Pallas kernels, body(): pl.pallas_call(filter_kernel, out_shape=jax.ShapeDtypeStruct((4, ROWS + 2...  124 us
    pallas_call x1, Pallas kernels, body(): pl.pallas_call(stencil_kernel, grid=(ROWS // BLOCK,), out_shape=(jax.Shap...  9.7 us
    unnamed x4, local copies, waits for them, and re-layouts  3.57 us

profile of v3, /device:TPU:97, one launch (start us, length us, event | category | flops | bytes accessed | tf_op | source)
XLA Modules:
  0.0 139.6 jit_solution(11585409539460406495)
XLA Ops:
  0.7 0.9 select_reduce_fusion
  1.6 0.9 broadcast_in_dim.26.lim_ref
  2.5 0.0 copy-start.1
  2.5 123.9 %polar_filter.1.state_ref = f32[4,92,16,384]{3,2,1,0:T(8,128)} custom-call(f32[2,90,16,360]{3,2,1,0:T(8,128)} %bitcast.6, f32[90,16,360]{2,1,0:T(8,128)} %bitcast.7, f32[90,16,360]{2,1,0:T(8,128)} %bitcast.8, f32[90,8,128]{2,1,0:T(8,128)} %broadcast_in_dim.26.lim_ref, f32[4,1,384]{2,1,0:T(1,128)} %constant.56.wv_ref, f32[2,384]{1,0:T(2,128)} %constant.43.clone.wp_ref, ...), custom_call_target="tpu_custom_call" | custom-call | tf_op jit(solution)/shard_map/polar_filter/pallas_call | solution.py:670
  126.3 0.0 copy-done.1
  126.4 0.0 copy-start
  126.4 3.6 %copy-done = f32[4,92,16,384]{3,2,1,0:T(8,128)S(1)} copy-done((f32[4,92,16,384]{3,2,1,0:T(8,128)S(1)}, f32[4,92,16,384]{3,2,1,0:T(8,128)}, u32[]{:S(2)}) %copy-start) | copy-done | bytes 9043992
  129.9 9.7 %stencil.1 = (f32[2,90,16,360]{3,2,1,0:T(8,128)}, f32[90,16,360]{2,1,0:T(8,128)}, f32[90,16,360]{2,1,0:T(8,128)}) custom-call(f32[3,1442]{1,0:T(4,128)S(1)} %copy-done.1, f32[4,92,16,384]{3,2,1,0:T(8,128)S(1)} %copy-done), custom_call_target="tpu_custom_call" | custom-call | tf_op jit(solution)/shard_map/stencil/pallas_call | solution.py:709
  (2 shorter events, 0.0 us)
Async XLA Ops:
  2.5 123.9 %copy-start.1 = (f32[3,1442]{1,0:T(4,128)S(1)}, f32[3,1442]{1,0:T(4,128)}, u32[]{:S(2)}) copy-start(f32[3,1442]{1,0:T(4,128)} %constant.52.clone.trig_ref) | copy-start | bytes 51916
  126.4 3.6 %copy-start = (f32[4,92,16,384]{3,2,1,0:T(8,128)S(1)}, f32[4,92,16,384]{3,2,1,0:T(8,128)}, u32[]{:S(2)}) copy-start(f32[4,92,16,384]{3,2,1,0:T(8,128)} %polar_filter.1.state_ref) | copy-start | bytes 27131908

commit v4 on v3

--- a/solution.py
+++ b/solution.py
@@ -19,9 +19,11 @@
 SUB = 8
 NCH = 9
 CR = ROWS // NCH
-OFF1 = 6
-OFF2 = 5
-MID = 5
+OFF1 = 5
+OFF2 = 4
+NSUB = 3
+SR = HALF // NSUB
+NG = 4
 BLOCK = 9
 MESH = pl.DeviceIdType.MESH
 F32 = jnp.float32
@@ -113,9 +115,9 @@
     thi_ref, tlo_ref, uhi_ref, ulo_ref, fhi_ref, flo_ref, ghi_ref, glo_ref,
     state_ref,
     thi, tlo, uhi, ulo, fhi, flo, ghi, glo,
-    recv, ret, strips, srecv, arecv, stage, obuf, xs, yb, zb, rawp, cols, side, zero, home,
+    recv, ret, srecv, stage, obuf, pbuf, xs, yb, zb, rawp, cols, side, zero, home,
     tab_sem, stage_sem, fsend, frecv, rsend, rrecv, ssend, srecv_sem, asend, arecv_sem,
-    hsend, hrecv, lsend, lrecv, osem, zsem, xsend, xrecv,
+    hsend, hrecv, lsend, lrecv, osem, zsem, xsend, xrecv, part_sem, psem,
 ):
     lat = lax.axis_index("lat")
     lon = lax.axis_index("lon")
@@ -153,8 +155,22 @@
         for i, (src, dst) in enumerate(packs):
             pltpu.make_async_copy(src.at[lon], dst, tab_sem.at[i]).start()
 
+    @pl.when(is_value | is_off)
+    def _():
+        for i, (src, dst) in enumerate(tables):
+            pltpu.make_async_copy(src, dst, tab_sem.at[i]).start()
+        yb[...] = jnp.zeros_like(yb)
+
     def part(g, rows):
         return sources[g // 2].at[rows, 8 * (g % 2) : 8 * (g % 2) + 8]
+
+    def whole_part(g):
+        return pltpu.make_async_copy(part(g, slice(0, ROWS)), recv.at[g], part_sem.at[g])
+
+    @pl.when(is_packed)
+    def _():
+        for g in range(NP):
+            whole_part(g).start()
 
     def stage_copy(g, slot):
         return pltpu.make_async_copy(part(g, slice(0, ROWS)), stage.at[slot], stage_sem.at[slot])
@@ -179,51 +195,34 @@
         for k in range(4):
             act(relay(c, k))
 
-    def relay_next(c, carry):
-        relay_all(c - 2, lambda copy: copy.wait_send())
-        relay_all(c, lambda copy: copy.start())
-        return carry
-
-    def relay_only(c, carry):
-        relay_all(c, lambda copy: copy.start())
-        return carry
-
-    @pl.when(is_value)
-    def _():
-        lax.fori_loop(0, jnp.minimum(n_off, 2), relay_only, 0)
-
-        def per_copy(n, carry):
-            c = first + n // NP
-            p = lax.rem(lon + n, NP)
-            dst = recv.at[c, lon]
-            for g in range(NP):
-                src = part(g, pl.ds(c * CR, CR))
-
-                @pl.when((p == g) & (p != lon))
+    def stay(c):
+        def per_owner(i, carry):
+            p = lax.rem(lon + i, NP)
+            dst = recv.at[lon, pl.ds(c * CR, CR)]
+            half = pl.ds(pl.multiple_of(lax.rem(p, 2) * 8, 8), 8)
+            for k in range(4):
+                src = sources[k].at[pl.ds(c * CR, CR), half]
+
+                @pl.when((p // 2 == k) & (p != lon))
                 def _(src=src):
                     pltpu.make_async_remote_copy(
                         src_ref=src, dst_ref=dst, send_sem=fsend.at[c, p],
                         recv_sem=frecv.at[c, lon], device_id=(lat, p), device_id_type=MESH,
                     ).start()
 
-                @pl.when((p == g) & (p == lon))
+                @pl.when((p // 2 == k) & (p == lon))
                 def _(src=src):
                     pltpu.make_async_copy(src, dst, frecv.at[c, lon]).start()
 
             return carry
 
-        lax.fori_loop(0, (last - first) * NP, per_copy, 0)
-
-    @pl.when(is_value | is_off)
-    def _():
-        for i, (src, dst) in enumerate(tables):
-            pltpu.make_async_copy(src, dst, tab_sem.at[i]).start()
-        yb[...] = jnp.zeros_like(yb)
-
-    def strip_copy(p):
+        lax.fori_loop(0, NP, per_owner, 0)
+
+    def strip_copy(p, sub):
+        rows = pl.ds(sub * SR, SR)
         return pltpu.make_async_remote_copy(
-            src_ref=strips.at[p], dst_ref=srecv.at[lon], send_sem=ssend.at[p],
-            recv_sem=srecv_sem.at[lon], device_id=(lat, p), device_id_type=MESH,
+            src_ref=ret.at[p, rows], dst_ref=srecv.at[lon, rows], send_sem=ssend.at[sub, p],
+            recv_sem=srecv_sem.at[sub, lon], device_id=(lat, p), device_id_type=MESH,
         )
 
     @pl.when(is_packed)
@@ -231,117 +230,132 @@
         xs[...] = jnp.zeros_like(xs)
         for i, (src, dst) in enumerate(packs):
             pltpu.make_async_copy(src.at[lon], dst, tab_sem.at[i]).wait()
-
-        def load_part(g, slot):
-            half = pl.ds(pl.multiple_of(lax.rem(g, 2) * 8, 8), 8)
-            for k in range(4):
-                @pl.when(g // 2 == k)
-                def _(k=k):
-                    pltpu.make_async_copy(sources[k].at[:, half], stage.at[slot], stage_sem.at[slot]).start()
-
-        load_part(lax.rem(lon + 1, NP), 0)
-
-        def ahead(i, carry):
-            g = lax.rem(lon + 1 + i, NP)
-            slot = lax.rem(i, 2)
-
-            @pl.when(i + 1 < NP)
-            def _():
-                load_part(lax.rem(g + 1, NP), 1 - slot)
-
-            pltpu.make_async_copy(stage.at[slot], stage.at[slot], stage_sem.at[slot]).wait()
-            xs[:, 0:COLS] = stage[slot].reshape(ROWS * SUB, COLS)
-            low = dot3(xs[0 : HALF * SUB, :], fhi[0], flo[0]).reshape(HALF, SUB, PC)
-            strips[g] = jnp.where(wp_ref[0:1, :] <= wide(lim_ref[0:HALF]), low, 0.0)
-            high = dot3(xs[HALF * SUB :, :], fhi[1], flo[1]).reshape(HALF, SUB, PC)
-            obuf[slot, 0:HALF] = jnp.where(wp_ref[1:2, :] <= wide(lim_ref[HALF:]), high, 0.0)
-
-            def pair(j, carry):
-                strips[g, j] += obuf[slot, HALF - 1 - j]
-                return carry
-
-            lax.fori_loop(0, HALF, pair, 0, unroll=9)
-
-            @pl.when(lon != g)
-            def _():
-                strip_copy(g).start()
-
-            @pl.when(lon == g)
-            def _():
-                pltpu.make_async_copy(strips.at[g], srecv.at[g], srecv_sem.at[g]).start()
-
-            return carry
-
-        lax.fori_loop(0, NP, ahead, 0)
-
-        def wait_part(s, carry):
-            pltpu.make_async_copy(srecv.at[s], srecv.at[s], srecv_sem.at[s]).wait()
-            return carry
-
-        lax.fori_loop(0, NP, wait_part, 0)
-
-        def add(i, carry):
-            total = srecv[0, i]
-            for s in range(1, NP):
-                total = total + srecv[s, i]
-            arecv[lon, i] = total
-            return carry
-
-        lax.fori_loop(0, HALF, add, 0, unroll=5)
-
-        def sum_to(p):
+        for g in range(NP):
+            whole_part(g).wait()
+
+        def keep(sub):
+            near = wp_ref[0:1, :] <= wide(lim_ref[pl.ds(sub * SR, SR)])
+            far = wp_ref[1:2, :] <= wide(lim_ref[pl.ds(ROWS - SR - sub * SR, SR)])
+            return near[None], far[None]
+
+        def ahead(n, carry):
+            sub = n // (NP // NG)
+            base = lon + 1 + lax.rem(n, NP // NG) * NG
+            for i in range(NG):
+                g = lax.rem(base + i, NP)
+                near = recv[g, pl.ds(sub * SR, SR)].reshape(SR * SUB, COLS)
+                far = recv[g, pl.ds(ROWS - SR - sub * SR, SR)].reshape(SR * SUB, COLS)
+                xs[0, i * SR * SUB : (i + 1) * SR * SUB, 0:COLS] = near
+                xs[1, i * SR * SUB : (i + 1) * SR * SUB, 0:COLS] = far
+            keep_near, keep_far = keep(sub)
+            shape = (NG, SR, SUB, PC)
+            pbuf[0, :, 0] = jnp.where(keep_near, dot3(xs[0], fhi[0], flo[0]).reshape(shape), 0.0)
+            pbuf[0, :, 1] = jnp.where(keep_far, dot3(xs[1], fhi[1], flo[1]).reshape(shape), 0.0)
+            for i in range(NG):
+                g = lax.rem(base + i, NP)
+                for j in range(SR):
+                    ret[g, sub * SR + j] = pbuf[0, i, 0, j] + pbuf[0, i, 1, SR - 1 - j]
+
+                @pl.when(lon != g)
+                def _(g=g):
+                    strip_copy(g, sub).start()
+
+                @pl.when(lon == g)
+                def _(g=g):
+                    rows = pl.ds(sub * SR, SR)
+                    pltpu.make_async_copy(ret.at[g, rows], srecv.at[g, rows], srecv_sem.at[sub, g]).start()
+
+            return carry
+
+        lax.fori_loop(0, NSUB * (NP // NG), ahead, 0)
+
+        def sum_rows(p, sub):
+            return ret.at[p, pl.ds(HALF + sub * SR, SR)]
+
+        def sum_to(p, sub):
             return pltpu.make_async_remote_copy(
-                src_ref=arecv.at[lon], dst_ref=arecv.at[lon], send_sem=asend.at[p],
-                recv_sem=arecv_sem.at[lon], device_id=(lat, p), device_id_type=MESH,
+                src_ref=sum_rows(lon, sub), dst_ref=sum_rows(lon, sub), send_sem=asend.at[sub, p],
+                recv_sem=arecv_sem.at[sub, lon], device_id=(lat, p), device_id_type=MESH,
             )
 
-        def send(i, carry):
-            sum_to(lax.rem(lon + i, NP)).start()
-            return carry
-
-        lax.fori_loop(1, NP, send, 0)
-
-        def out_copy(p, slot):
-            return pltpu.make_async_copy(obuf.at[slot], state_part(p, 1, ROWS), osem.at[slot])
-
-        def back(i, carry):
-            g = lax.rem(lon + i, NP)
-            slot = lax.rem(i, 2)
-
-            @pl.when(i > 0)
-            def _():
-                pltpu.make_async_copy(arecv.at[g], arecv.at[g], arecv_sem.at[g]).wait()
-
-            @pl.when(i >= 2)
-            def _():
-                out_copy(g, slot).wait()
-
-            spec = arecv[g]
-            low = jnp.where(wp_ref[0:1, :] <= wide(lim_ref[0:HALF]), spec, 0.0).reshape(HALF * SUB, PC)
-            obuf[slot, 0:HALF] = dot3(low, ghi[0], glo[0]).reshape(HALF, SUB, PC)
-
-            def flip(j, carry):
-                xs[pl.ds(pl.multiple_of(j * SUB, SUB), SUB), :] = arecv[g, HALF - 1 - j]
-                return carry
-
-            lax.fori_loop(0, HALF, flip, 0, unroll=9)
-            high = xs[0 : HALF * SUB, :].reshape(HALF, SUB, PC)
-            high = jnp.where(wp_ref[1:2, :] <= wide(lim_ref[HALF:]), high, 0.0).reshape(HALF * SUB, PC)
-            obuf[slot, HALF:ROWS] = dot3(high, ghi[1], glo[1]).reshape(HALF, SUB, PC)
-            out_copy(g, slot).start()
-            return carry
-
-        lax.fori_loop(0, NP, back, 0)
-        for slot in range(2):
-            out_copy(0, slot).wait()
-
-        def sent(i, carry):
-            p = lax.rem(lon + i, NP)
-            sum_to(p).wait_send()
-            strip_copy(p).wait_send()
-            return carry
-
-        lax.fori_loop(1, NP, sent, 0)
+        def add_up(sub, carry):
+            def wait_part(p, carry):
+                ref = srecv.at[p, pl.ds(sub * SR, SR)]
+                pltpu.make_async_copy(ref, ref, srecv_sem.at[sub, p]).wait()
+                return carry
+
+            lax.fori_loop(0, NP, wait_part, 0)
+
+            def add(j, carry):
+                total = srecv[0, sub * SR + j]
+                for p in range(1, NP):
+                    total = total + srecv[p, sub * SR + j]
+                ret[lon, HALF + sub * SR + j] = total
+                return carry
+
+            lax.fori_loop(0, SR, add, 0, unroll=5)
+
+            def send(i, carry):
+                sum_to(lax.rem(lon + i, NP), sub).start()
+                return carry
+
+            lax.fori_loop(1, NP, send, 0)
+            return carry
+
+        lax.fori_loop(0, NSUB, add_up, 0)
+
+        def out_copies(n, act):
+            slot = lax.rem(n, 2)
+            sub = n // (NP // NG)
+            base = lon + lax.rem(n, NP // NG) * NG
+            for i in range(NG):
+                g = lax.rem(base + i, NP)
+                for far in range(2):
+                    start = ROWS - SR - sub * SR if far else sub * SR
+                    act(pltpu.make_async_copy(
+                        pbuf.at[slot, i, far], state_part(g, 1 + start, SR), psem.at[slot, i, far]
+                    ))
+
+        def back(n, carry):
+            slot = lax.rem(n, 2)
+            sub = n // (NP // NG)
+            base = lon + lax.rem(n, NP // NG) * NG
+            for i in range(NG):
+                g = lax.rem(base + i, NP)
+
+                @pl.when(g != lon)
+                def _(g=g):
+                    pltpu.make_async_copy(sum_rows(g, sub), sum_rows(g, sub), arecv_sem.at[sub, g]).wait()
+
+                for j in range(SR):
+                    spec = ret[g, HALF + sub * SR + j]
+                    xs[0, (i * SR + j) * SUB : (i * SR + j + 1) * SUB, :] = spec
+                    xs[1, (i * SR + SR - 1 - j) * SUB : (i * SR + SR - j) * SUB, :] = spec
+
+            @pl.when(n >= 2)
+            def _():
+                out_copies(n - 2, lambda copy: copy.wait())
+
+            shape = (NG, SR, SUB, PC)
+            for far, keep_it in enumerate(keep(sub)):
+                spec = jnp.where(keep_it, xs[far].reshape(shape), 0.0).reshape(NG * SR * SUB, PC)
+                pbuf[slot, :, far] = dot3(spec, ghi[far], glo[far]).reshape(shape)
+            out_copies(n, lambda copy: copy.start())
+            return carry
+
+        steps = NSUB * (NP // NG)
+        lax.fori_loop(0, steps, back, 0)
+        for n in (steps - 2, steps - 1):
+            out_copies(n, lambda copy: copy.wait())
+
+        def sent(n, carry):
+            sub = n // (NP - 1)
+            p = lax.rem(lon + 1 + lax.rem(n, NP - 1), NP)
+            sum_to(p, sub).wait_send()
+            strip_copy(p, sub).wait_send()
+            return carry
+
+        lax.fori_loop(0, NSUB * (NP - 1), sent, 0)
 
     @pl.when(depth >= 3)
     def _():
@@ -417,21 +431,19 @@
 
     @pl.when(is_value | is_off)
     def _():
-        for i, (src, dst) in enumerate(tables):
-            pltpu.make_async_copy(src, dst, tab_sem.at[i]).wait()
-
         half = np.float32(np.sqrt(0.5))
 
         def chunk(c, carry):
             def arrived(s, carry):
-                pltpu.make_async_copy(recv.at[c, s], recv.at[c, s], frecv.at[c, s]).wait()
+                ref = recv.at[s, pl.ds(c * CR, CR)]
+                pltpu.make_async_copy(ref, ref, frecv.at[c, s]).wait()
                 return carry
 
             lax.fori_loop(0, NP, arrived, 0)
 
             def fold(r, carry):
                 rows = pl.ds(pl.multiple_of(r * SUB, SUB), SUB)
-                x = [recv[c, s, r] for s in range(NP)]
+                x = [recv[s, c * CR + r] for s in range(NP)]
                 s0, s1, s2, s3 = [x[j] + x[j + 4] for j in range(4)]
                 d0, d1, d2, d3 = [x[j] - x[j + 4] for j in range(4)]
                 plus, minus = half * (d1 + d3), half * (d1 - d3)
@@ -464,8 +476,8 @@
                 even = (a0 + b0 + a2, a0 - b0 - b2, a0 + b0 - a2, a0 - b0 + b2)
                 odd = (a1 + a3, half * ((a1 - a3) - (b1 + b3)), b3 - b1, half * ((a3 - a1) - (b1 + b3)))
                 for j in range(4):
-                    ret[c, j, r] = even[j] + odd[j]
-                    ret[c, j + 4, r] = even[j] - odd[j]
+                    ret[j, c * CR + r] = even[j] + odd[j]
+                    ret[j + 4, c * CR + r] = even[j] - odd[j]
                 return carry
 
             lax.fori_loop(0, CR, unfold, 0)
@@ -477,33 +489,34 @@
                 def select(r, carry):
                     listed = wide(lim_ref[c * CR + r]) >= 0.0
                     for p in range(NP):
-                        rawp[p, :, 0:COLS] = recv[c, p, r]
+                        rawp[p, :, 0:COLS] = recv[p, c * CR + r]
                     for p in range(NP):
-                        east = recv[c, (p + 1) % NP, r, :, 0:1]
-                        west = recv[c, (p + 7) % NP, r, :, COLS - 1 : COLS]
+                        east = recv[(p + 1) % NP, c * CR + r, :, 0:1]
+                        west = recv[(p + 7) % NP, c * CR + r, :, COLS - 1 : COLS]
                         tail = jnp.where(lane == COLS - 256, east, rawp[p, :, 256:PC])
                         tail = jnp.where(lane == 127, west, tail)
                         raw = jnp.concatenate([rawp[p, :, 0:256], tail], axis=-1)
-                        ret[c, p, r] = jnp.where(listed, ret[c, p, r], raw)
+                        ret[p, c * CR + r] = jnp.where(listed, ret[p, c * CR + r], raw)
                     return carry
 
                 lax.fori_loop(0, CR, select, 0)
 
             def give_back(i, carry):
                 p = lax.rem(lon + i, NP)
+                src = ret.at[p, pl.ds(c * CR, CR)]
                 dst = state_part(lon, 1 + c * CR, CR)
                 local = is_value & (p == lon)
 
                 @pl.when(jnp.logical_not(local))
                 def _():
                     pltpu.make_async_remote_copy(
-                        src_ref=ret.at[c, p], dst_ref=dst, send_sem=rsend.at[c, p],
+                        src_ref=src, dst_ref=dst, send_sem=rsend.at[c, p],
                         recv_sem=rrecv.at[c, lon], device_id=(served, p), device_id_type=MESH,
                     ).start()
 
                 @pl.when(local)
                 def _():
-                    pltpu.make_async_copy(ret.at[c, p], dst, rrecv.at[c, lon]).start()
+                    pltpu.make_async_copy(src, dst, rrecv.at[c, lon]).start()
 
                 return carry
 
@@ -512,7 +525,7 @@
 
         def pass_on(c):
             relay_all(c, lambda copy: copy.wait_recv())
-            dst = recv.at[c, lon]
+            dst = recv.at[lon, pl.ds(c * CR, CR)]
 
             def home_part(p):
                 return home.at[c, p // 2, :, pl.ds(pl.multiple_of(lax.rem(p, 2) * 8, 8), 8)]
@@ -528,26 +541,39 @@
             lax.fori_loop(1, NP, to_owner, 0)
             pltpu.make_async_copy(home_part(lon), dst, frecv.at[c, lon]).start()
 
+        n_loc = last - first
+
         def step(n, carry):
-            @pl.when(is_off & (n < last))
+            @pl.when(is_value & (n < n_off))
+            def _():
+                @pl.when(n >= 2)
+                def _():
+                    relay_all(n - 2, lambda copy: copy.wait_send())
+
+                relay_all(n, lambda copy: copy.start())
+
+            @pl.when(is_value & (n < n_loc))
+            def _():
+                stay(first + n)
+
+            @pl.when(is_off & (n < n_off))
             def _():
                 pass_on(n)
 
-            @pl.when(n > first)
-            def _():
-                chunk(n - 1, 0)
-
-            return carry
-
-        @pl.when(is_value)
-        def _():
-            lax.fori_loop(2, jnp.minimum(n_off, MID), relay_next, 0)
-
-        lax.fori_loop(first, last + 1, step, 0)
-
-        @pl.when(is_value)
-        def _():
-            lax.fori_loop(MID, n_off, relay_next, 0)
+            @pl.when(n == 1)
+            def _():
+                for i, (src, dst) in enumerate(tables):
+                    pltpu.make_async_copy(src, dst, tab_sem.at[i]).wait()
+
+            lag = jnp.where(is_off, 1, 2)
+
+            @pl.when((n >= lag) & (n < n_loc + lag))
+            def _():
+                chunk(first + n - lag, 0)
+
+            return carry
+
+        lax.fori_loop(0, jnp.where(is_off, n_off + 1, jnp.maximum(n_off, n_loc + 2)), step, 0)
 
         def returned(n, carry):
             c = first + n // NP
@@ -555,11 +581,13 @@
 
             @pl.when(is_off | (p != lon))
             def _():
-                pltpu.make_async_copy(ret.at[c, p], ret.at[c, p], rsend.at[c, p]).wait()
+                ref = ret.at[p, pl.ds(c * CR, CR)]
+                pltpu.make_async_copy(ref, ref, rsend.at[c, p]).wait()
 
             @pl.when(p != lon)
             def _():
-                pltpu.make_async_copy(recv.at[c, p], recv.at[c, p], fsend.at[c, p]).wait()
+                ref = recv.at[p, pl.ds(c * CR, CR)]
+                pltpu.make_async_copy(ref, ref, fsend.at[c, p]).wait()
 
             return carry
 
@@ -677,14 +705,13 @@
             pltpu.VMEM((4, PC, 2 * PC), BF16), pltpu.VMEM((4, PC, 2 * PC), BF16),
             pltpu.VMEM((2, PC, PC), BF16), pltpu.VMEM((2, PC, PC), BF16),
             pltpu.VMEM((2, PC, PC), BF16), pltpu.VMEM((2, PC, PC), BF16),
-            pltpu.VMEM((NCH, NP, CR, SUB, COLS), F32),
-            pltpu.VMEM((NCH, NP, CR, SUB, PC), F32),
-            pltpu.VMEM((NP, HALF, SUB, PC), F32),
-            pltpu.VMEM((NP, HALF, SUB, PC), F32),
+            pltpu.VMEM((NP, ROWS, SUB, COLS), F32),
+            pltpu.VMEM((NP, ROWS, SUB, PC), F32),
             pltpu.VMEM((NP, HALF, SUB, PC), F32),
             pltpu.VMEM((2, ROWS, SUB, COLS), F32),
             pltpu.VMEM((2, ROWS, SUB, PC), F32),
-            pltpu.VMEM((ROWS * SUB, PC), F32),
+            pltpu.VMEM((2, NG, 2, SR, SUB, PC), F32),
+            pltpu.VMEM((2, NG * SR * SUB, PC), F32),
             pltpu.VMEM((8, CR * SUB, PC), F32),
             pltpu.VMEM((8, CR * SUB, PC), F32),
             pltpu.VMEM((NP, SUB, PC), F32),
@@ -694,9 +721,9 @@
             pltpu.VMEM((max(OFF1, OFF2), 4, CR, LEV, COLS), F32),
             dma((4,)), dma((2,)),
             dma((NCH, NP)), dma((NCH, NP)), dma((NCH, NP)), dma((NCH, NP)),
-            dma((NP,)), dma((NP,)), dma((NP,)), dma((NP,)),
+            dma((NSUB, NP)), dma((NSUB, NP)), dma((NSUB, NP)), dma((NSUB, NP)),
             dma((2,)), dma((2,)), dma((2,)), dma((2,)), dma((2,)), dma,
-            dma((NCH, 4)), dma((NCH, 4)),
+            dma((NCH, 4)), dma((NCH, 4)), dma((NP,)), dma((2, NG, 2)),
         ],
         compiler_params=pltpu.CompilerParams(
             collective_id=1, has_side_effects=True, vmem_limit_bytes=60 * 2**20
@@ -726,7 +753,7 @@
             pl.BlockSpec((BLOCK, LEV, COLS), lambda i: (i, 0, 0)),
             pl.BlockSpec((BLOCK, LEV, COLS), lambda i: (i, 0, 0)),
         ),
-        compiler_params=pltpu.CompilerParams(vmem_limit_bytes=32 * 2**20),
+        compiler_params=pltpu.CompilerParams(vmem_limit_bytes=60 * 2**20),
         name="stencil",
     )(jnp.asarray(trig_table()), state)
     return new_winds.transpose(0, 2, 1, 3), new_t.transpose(1, 0, 2), new_h.transpose(1, 0, 2)

time: 140 us -> 128 us (0.914)
  the two profiles are of different devices: /device:TPU:97 before, /device:TPU:11 now
where the time goes in v4:
time: 128 us; the launch traced here: 127 us
  Pallas kernels  125 us (98%)
    pallas_call x1, Pallas kernels, body(): pl.pallas_call(filter_kernel, out_shape=jax.ShapeDtypeStruct((4, ROWS + 2...  112 us
    pallas_call x1, Pallas kernels, body(): pl.pallas_call(stencil_kernel, grid=(ROWS // BLOCK,), out_shape=(jax.Shap...  12.7 us

profile of v4, /device:TPU:11, one launch (start us, length us, event | category | flops | bytes accessed | tf_op | source)
XLA Modules:
  0.0 127.3 jit_solution(8385970907493748118)
XLA Ops:
  0.7 0.9 select_reduce_fusion
  1.6 0.9 broadcast_in_dim.26.lim_ref
  2.5 112.1 %polar_filter.1.state_ref = f32[4,92,16,384]{3,2,1,0:T(8,128)} custom-call(f32[2,90,16,360]{3,2,1,0:T(8,128)} %bitcast.6, f32[90,16,360]{2,1,0:T(8,128)} %bitcast.7, f32[90,16,360]{2,1,0:T(8,128)} %bitcast.8, f32[90,8,128]{2,1,0:T(8,128)} %broadcast_in_dim.26.lim_ref, f32[4,1,384]{2,1,0:T(1,128)} %constant.56.wv_ref, f32[2,384]{1,0:T(2,128)} %constant.43.clone.wp_ref, ...), custom_call_target="tpu_custom_call" | custom-call | tf_op jit(solution)/shard_map/polar_filter/pallas_call | solution.py:698
  114.6 12.7 %stencil.1 = (f32[2,90,16,360]{3,2,1,0:T(8,128)}, f32[90,16,360]{2,1,0:T(8,128)}, f32[90,16,360]{2,1,0:T(8,128)}) custom-call(f32[3,1442]{1,0:T(4,128)} %constant.52.clone.trig_ref, f32[4,92,16,384]{3,2,1,0:T(8,128)} %polar_filter.1.state_ref), custom_call_target="tpu_custom_call" | custom-call | tf_op jit(solution)/shard_map/stencil/pallas_call | solution.py:736
  (2 shorter events, 0.0 us)

commit v5 on v4

--- a/solution.py
+++ b/solution.py
@@ -17,14 +17,14 @@
 PC = 384
 NP = 8
 SUB = 8
-NCH = 9
+NCH = 15
 CR = ROWS // NCH
-OFF1 = 5
-OFF2 = 4
+OFF1 = 10
+OFF2 = 7
 NSUB = 3
 SR = HALF // NSUB
 NG = 4
-BLOCK = 9
+BLOCK = 18
 MESH = pl.DeviceIdType.MESH
 F32 = jnp.float32
 BF16 = jnp.bfloat16
@@ -101,9 +101,9 @@
 def dot3(x, hi, lo):
     x_hi = x.astype(BF16)
     x_lo = (x - x_hi.astype(F32)).astype(BF16)
-    total = jnp.dot(x_hi, lo, preferred_element_type=F32)
-    total += jnp.dot(x_lo, hi, preferred_element_type=F32)
-    return total + jnp.dot(x_hi, hi, preferred_element_type=F32)
+    count = x.shape[0]
+    both = jnp.dot(jnp.concatenate([x_lo, x_hi], axis=0), hi, preferred_element_type=F32)
+    return jnp.dot(x_hi, lo, preferred_element_type=F32) + both[:count] + both[count:]
 
 
 def wide(lim):
@@ -357,6 +357,58 @@
 
         lax.fori_loop(0, NSUB * (NP - 1), sent, 0)
 
+    def side_copy(i):
+        step = NP - 1 if i == 0 else 1
+        return pltpu.make_async_remote_copy(
+            src_ref=cols.at[i], dst_ref=side.at[i], send_sem=hsend.at[i], recv_sem=hrecv.at[i],
+            device_id=(lat, lax.rem(lon + step, NP)), device_id_type=MESH,
+        )
+
+    own_start = jnp.where(lat == 3, ROWS // 3, 0)
+
+    def raw_copy(g, slot, act):
+        full = pltpu.make_async_copy(obuf.at[slot], state_part(g, 1, ROWS), osem.at[slot])
+        some = pltpu.make_async_copy(
+            obuf.at[slot, pl.ds(own_start, 2 * ROWS // 3)],
+            state_part(g, 1 + own_start, 2 * ROWS // 3), osem.at[slot],
+        )
+
+        @pl.when(depth > 3)
+        def _():
+            act(full)
+
+        @pl.when(depth == 3)
+        def _():
+            act(some)
+
+    def raw_out(g, carry):
+        slot = lax.rem(g, 2)
+        half = pl.ds(pl.multiple_of(slot * 8, 8), 8)
+        for k in range(4):
+            @pl.when(g // 2 == k)
+            def _(k=k):
+                pltpu.make_async_copy(sources[k].at[:, half], stage.at[slot], stage_sem.at[slot]).start()
+
+        @pl.when(g >= 2)
+        def _():
+            raw_copy(g - 2, slot, lambda copy: copy.wait())
+
+        pltpu.make_async_copy(stage.at[slot], stage.at[slot], stage_sem.at[slot]).wait()
+        lane = lax.broadcasted_iota(jnp.int32, (SUB, 128), 1)
+
+        def insert(j, carry):
+            obuf[slot, j, :, 0:COLS] = stage[slot, j]
+            east = pltpu.roll(side[0, g], lax.rem(COLS - 256 + 128 - j, 128), 1)
+            west = pltpu.roll(side[1, g], 127 - j, 1)
+            tail = obuf[slot, j, :, 256:PC]
+            tail = jnp.where(lane == COLS - 256, east, tail)
+            obuf[slot, j, :, 256:PC] = jnp.where(lane == 127, west, tail)
+            return carry
+
+        lax.fori_loop(0, ROWS, insert, 0, unroll=9)
+        raw_copy(g, slot, lambda copy: copy.start())
+        return carry
+
     @pl.when(depth >= 3)
     def _():
         lane = lax.broadcasted_iota(jnp.int32, (SUB, 128), 1)
@@ -377,57 +429,14 @@
             cols[0, g] = head
             cols[1, g] = tail
 
-        def side_copy(i):
-            step = NP - 1 if i == 0 else 1
-            return pltpu.make_async_remote_copy(
-                src_ref=cols.at[i], dst_ref=side.at[i], send_sem=hsend.at[i], recv_sem=hrecv.at[i],
-                device_id=(lat, lax.rem(lon + step, NP)), device_id_type=MESH,
-            )
-
         for i in range(2):
             side_copy(i).start()
-        stage_copy(0, 0).start()
-        for i in range(2):
-            side_copy(i).wait()
-
-        own_start = jnp.where(lat == 3, ROWS // 3, 0)
-
-        def out_copy(g, slot, act):
-            full = pltpu.make_async_copy(obuf.at[slot], state_part(g, 1, ROWS), osem.at[slot])
-            some = pltpu.make_async_copy(
-                obuf.at[slot, pl.ds(own_start, 2 * ROWS // 3)],
-                state_part(g, 1 + own_start, 2 * ROWS // 3), osem.at[slot],
-            )
-
-            @pl.when(depth > 3)
-            def _():
-                act(full)
-
-            @pl.when(depth == 3)
-            def _():
-                act(some)
-
-        for g in range(NP):
-            slot = g % 2
-            if g + 1 < NP:
-                stage_copy(g + 1, 1 - slot).start()
-            stage_copy(g, slot).wait()
-            if g >= 2:
-                out_copy(g, slot, lambda copy: copy.wait())
-
-            def insert(j, carry, g=g, slot=slot):
-                obuf[slot, j, :, 0:COLS] = stage[slot, j]
-                east = pltpu.roll(side[0, g], lax.rem(COLS - 256 + 128 - j, 128), 1)
-                west = pltpu.roll(side[1, g], 127 - j, 1)
-                tail = obuf[slot, j, :, 256:PC]
-                tail = jnp.where(lane == COLS - 256, east, tail)
-                obuf[slot, j, :, 256:PC] = jnp.where(lane == 127, west, tail)
-                return carry
-
-            lax.fori_loop(0, ROWS, insert, 0, unroll=9)
-            out_copy(g, slot, lambda copy: copy.start())
-        for slot in range(2):
-            out_copy(0, slot, lambda copy: copy.wait())
+
+        @pl.when(jnp.logical_not(is_off))
+        def _():
+            for i in range(2):
+                side_copy(i).wait()
+            lax.fori_loop(0, NP, raw_out, 0)
 
     @pl.when(is_value | is_off)
     def _():
@@ -457,7 +466,7 @@
                     yb[i, rows, 0:COLS] = out[i]
                 return carry
 
-            lax.fori_loop(0, CR, fold, 0)
+            lax.fori_loop(0, CR, fold, 0, unroll=3)
             limit = wide(lim_ref[pl.ds(c * CR, CR)])
 
             def group(g, carry):
@@ -480,7 +489,7 @@
                     ret[j + 4, c * CR + r] = even[j] - odd[j]
                 return carry
 
-            lax.fori_loop(0, CR, unfold, 0)
+            lax.fori_loop(0, CR, unfold, 0, unroll=3)
 
             @pl.when(served_depth >= 2)
             def _():
@@ -499,7 +508,7 @@
                         ret[p, c * CR + r] = jnp.where(listed, ret[p, c * CR + r], raw)
                     return carry
 
-                lax.fori_loop(0, CR, select, 0)
+                lax.fori_loop(0, CR, select, 0, unroll=2)
 
             def give_back(i, carry):
                 p = lax.rem(lon + i, NP)
@@ -571,6 +580,15 @@
             def _():
                 chunk(first + n - lag, 0)
 
+            @pl.when(is_off & (n >= 1))
+            def _():
+                @pl.when(n == 1)
+                def _():
+                    for i in range(2):
+                        side_copy(i).wait()
+
+                lax.fori_loop(jnp.minimum(n - 1, NP), jnp.where(n == n_off, NP, jnp.minimum(n, NP)), raw_out, 0)
+
             return carry
 
         lax.fori_loop(0, jnp.where(is_off, n_off + 1, jnp.maximum(n_off, n_loc + 2)), step, 0)
@@ -610,6 +628,11 @@
             return carry
 
         lax.fori_loop(jnp.maximum(n_off - 2, 0), n_off, relayed, 0)
+
+    @pl.when(depth >= 3)
+    def _():
+        for slot in range(2):
+            raw_copy(slot, slot, lambda copy: copy.wait())
 
     def edge_copy(i):
         row, there, step = ((1, ROWS + 1, 15), (ROWS, 0, 1))[i]

time: 128 us -> 125 us (0.977)
  the two profiles are of different devices: /device:TPU:11 before, /device:TPU:97 now
where the time goes in v5:
time: 125 us
  Pallas kernels  122 us (98%)
    pallas_call x1, Pallas kernels, body(): pl.pallas_call(filter_kernel, out_shape=jax.ShapeDtypeStruct((4, ROWS + 2...  111 us
    pallas_call x1, Pallas kernels, body(): pl.pallas_call(stencil_kernel, grid=(ROWS // BLOCK,), out_shape=(jax.Shap...  10.9 us

profile of v5, /device:TPU:97, one launch (start us, length us, event | category | flops | bytes accessed | tf_op | source)
XLA Modules:
  0.0 124.5 jit_solution(4375547214107272761)
XLA Ops:
  0.7 0.9 select_reduce_fusion
  1.6 0.9 broadcast_in_dim.26.lim_ref
  2.5 111.2 %polar_filter.1.state_ref = f32[4,92,16,384]{3,2,1,0:T(8,128)} custom-call(f32[2,90,16,360]{3,2,1,0:T(8,128)} %bitcast.6, f32[90,16,360]{2,1,0:T(8,128)} %bitcast.7, f32[90,16,360]{2,1,0:T(8,128)} %bitcast.8, f32[90,8,128]{2,1,0:T(8,128)} %broadcast_in_dim.26.lim_ref, f32[4,1,384]{2,1,0:T(1,128)} %constant.56.wv_ref, f32[2,384]{1,0:T(2,128)} %constant.43.clone.wp_ref, ...), custom_call_target="tpu_custom_call" | custom-call | tf_op jit(solution)/shard_map/polar_filter/pallas_call | solution.py:721
  113.7 10.9 %stencil.1 = (f32[2,90,16,360]{3,2,1,0:T(8,128)}, f32[90,16,360]{2,1,0:T(8,128)}, f32[90,16,360]{2,1,0:T(8,128)}) custom-call(f32[3,1442]{1,0:T(4,128)} %constant.52.clone.trig_ref, f32[4,92,16,384]{3,2,1,0:T(8,128)} %polar_filter.1.state_ref), custom_call_target="tpu_custom_call" | custom-call | tf_op jit(solution)/shard_map/stencil/pallas_call | solution.py:759
  (2 shorter events, 0.0 us)

commit v6 on v5

--- a/solution.py
+++ b/solution.py
@@ -218,6 +218,22 @@
 
         lax.fori_loop(0, NP, per_owner, 0)
 
+    def edge_copy(i):
+        row, there, step = ((1, ROWS + 1, 15), (ROWS, 0, 1))[i]
+        return pltpu.make_async_remote_copy(
+            src_ref=state_ref.at[:, row], dst_ref=state_ref.at[:, there],
+            send_sem=lsend.at[i], recv_sem=lrecv.at[i],
+            device_id=(lax.rem(lat + step, 16), lon), device_id_type=MESH,
+        )
+
+    inner = (lat > 0, lat < 15)
+
+    def edges_out():
+        for i in range(2):
+            @pl.when(inner[i])
+            def _(i=i):
+                edge_copy(i).start()
+
     def strip_copy(p, sub):
         rows = pl.ds(sub * SR, SR)
         return pltpu.make_async_remote_copy(
@@ -336,6 +352,10 @@
             def _():
                 out_copies(n - 2, lambda copy: copy.wait())
 
+            @pl.when(n == 4)
+            def _():
+                edges_out()
+
             shape = (NG, SR, SUB, PC)
             for far, keep_it in enumerate(keep(sub)):
                 spec = jnp.where(keep_it, xs[far].reshape(shape), 0.0).reshape(NG * SR * SUB, PC)
@@ -611,17 +631,30 @@
 
         lax.fori_loop(0, (last - first) * NP, returned, 0)
 
+    @pl.when(depth >= 3)
+    def _():
+        for slot in range(2):
+            raw_copy(slot, slot, lambda copy: copy.wait())
+
     @pl.when(is_value)
     def _():
-        def drain(n, carry):
-            c = begin + n // NP
-            p = lax.rem(n, NP)
-
-            dst = state_part(p, 1 + c * CR, CR)
-            pltpu.make_async_copy(dst, dst, rrecv.at[c, p]).wait()
-            return carry
-
-        lax.fori_loop(0, (end - begin) * NP, drain, 0)
+        def drain(m, carry):
+            c = jnp.where(m == 0, begin, jnp.where(m == 1, end - 1, begin + m - 1))
+
+            def one(p, carry):
+                dst = state_part(p, 1 + c * CR, CR)
+                pltpu.make_async_copy(dst, dst, rrecv.at[c, p]).wait()
+                return carry
+
+            lax.fori_loop(0, NP, one, 0)
+
+            @pl.when(m == 1)
+            def _():
+                edges_out()
+
+            return carry
+
+        lax.fori_loop(0, end - begin, drain, 0)
 
         def relayed(c, carry):
             relay_all(c, lambda copy: copy.wait_send())
@@ -629,27 +662,12 @@
 
         lax.fori_loop(jnp.maximum(n_off - 2, 0), n_off, relayed, 0)
 
-    @pl.when(depth >= 3)
-    def _():
-        for slot in range(2):
-            raw_copy(slot, slot, lambda copy: copy.wait())
-
-    def edge_copy(i):
-        row, there, step = ((1, ROWS + 1, 15), (ROWS, 0, 1))[i]
-        return pltpu.make_async_remote_copy(
-            src_ref=state_ref.at[:, row], dst_ref=state_ref.at[:, there],
-            send_sem=lsend.at[i], recv_sem=lrecv.at[i],
-            device_id=(lax.rem(lat + step, 16), lon), device_id_type=MESH,
-        )
-
     def blank(row):
         return pltpu.make_async_copy(zero, state_ref.at[:, row], zsem)
 
-    inner = (lat > 0, lat < 15)
-    for i in range(2):
-        @pl.when(inner[i])
-        def _(i=i):
-            edge_copy(i).start()
+    @pl.when(depth >= 4)
+    def _():
+        edges_out()
 
     for i, row in ((0, 0), (1, ROWS + 1)):
         @pl.when(jnp.logical_not(inner[i]))

time: 125 us -> 123 us (0.984)
  the two profiles are of different devices: /device:TPU:97 before, /device:TPU:89 now
where the time goes in v6:
time: 123 us; the launch traced here: 122 us
  Pallas kernels  119 us (97%)
    pallas_call x1, Pallas kernels, body(): pl.pallas_call(filter_kernel, out_shape=jax.ShapeDtypeStruct((4, ROWS + 2...  108 us
    pallas_call x1, Pallas kernels, body(): pl.pallas_call(stencil_kernel, grid=(ROWS // BLOCK,), out_shape=(jax.Shap...  10.9 us

profile of v6, /device:TPU:89, one launch (start us, length us, event | category | flops | bytes accessed | tf_op | source)
XLA Modules:
  0.0 121.8 jit_solution(475349306955471413)
XLA Ops:
  0.7 0.9 select_reduce_fusion
  1.6 0.9 broadcast_in_dim.26.lim_ref
  2.5 108.5 %polar_filter.1.state_ref = f32[4,92,16,384]{3,2,1,0:T(8,128)} custom-call(f32[2,90,16,360]{3,2,1,0:T(8,128)} %bitcast.6, f32[90,16,360]{2,1,0:T(8,128)} %bitcast.7, f32[90,16,360]{2,1,0:T(8,128)} %bitcast.8, f32[90,8,128]{2,1,0:T(8,128)} %broadcast_in_dim.26.lim_ref, f32[4,1,384]{2,1,0:T(1,128)} %constant.56.wv_ref, f32[2,384]{1,0:T(2,128)} %constant.43.clone.wp_ref, ...), custom_call_target="tpu_custom_call" | custom-call | tf_op jit(solution)/shard_map/polar_filter/pallas_call | solution.py:739
  111.0 10.9 %stencil.1 = (f32[2,90,16,360]{3,2,1,0:T(8,128)}, f32[90,16,360]{2,1,0:T(8,128)}, f32[90,16,360]{2,1,0:T(8,128)}) custom-call(f32[3,1442]{1,0:T(4,128)} %constant.52.clone.trig_ref, f32[4,92,16,384]{3,2,1,0:T(8,128)} %polar_filter.1.state_ref), custom_call_target="tpu_custom_call" | custom-call | tf_op jit(solution)/shard_map/stencil/pallas_call | solution.py:777
  (2 shorter events, 0.0 us)

commit v7 on v6

--- a/solution.py
+++ b/solution.py
@@ -111,10 +111,10 @@
 
 
 def filter_kernel(
-    w_ref, t_ref, h_ref, lim_ref, wv_ref, wp_ref,
+    w_ref, t_ref, h_ref, cut_ref, wv_ref, wp_ref,
     thi_ref, tlo_ref, uhi_ref, ulo_ref, fhi_ref, flo_ref, ghi_ref, glo_ref,
     state_ref,
-    thi, tlo, uhi, ulo, fhi, flo, ghi, glo,
+    lim_ref, thi, tlo, uhi, ulo, fhi, flo, ghi, glo,
     recv, ret, srecv, stage, obuf, pbuf, xs, yb, zb, rawp, cols, side, zero, home,
     tab_sem, stage_sem, fsend, frecv, rsend, rrecv, ssend, srecv_sem, asend, arecv_sem,
     hsend, hrecv, lsend, lrecv, osem, zsem, xsend, xrecv, part_sem, psem,
@@ -182,6 +182,11 @@
     def _():
         stage_copy(0, 0).start()
 
+    def spread(j, carry):
+        lim_ref[j] = jnp.full((SUB, 128), cut_ref[j], F32)
+        return carry
+
+    lax.fori_loop(0, ROWS, spread, 0, unroll=6)
     pl.semaphore_wait(bar, n_signals)
 
     def relay(c, k):
@@ -730,7 +735,6 @@
     rows = served * ROWS + jnp.arange(ROWS, dtype=jnp.int32)
     hits = polar_rows[None, :] == rows[:, None]
     limit = jnp.max(jnp.where(hits, cutoffs[None, :], -1), axis=1).astype(F32)
-    lim = jnp.broadcast_to(limit[:, None, None], (ROWS, SUB, 128))
     thi, tlo, uhi, ulo, wv = value_tables()
     fhi, flo, ghi, glo, wp = packed_tables()
     vm = pl.BlockSpec(memory_space=pltpu.VMEM)
@@ -739,9 +743,10 @@
     state = pl.pallas_call(
         filter_kernel,
         out_shape=jax.ShapeDtypeStruct((4, ROWS + 2, LEV, PC), F32),
-        in_specs=[hbm, hbm, hbm, vm, vm, vm] + [hbm] * 8,
+        in_specs=[hbm, hbm, hbm, pl.BlockSpec(memory_space=pltpu.SMEM), vm, vm] + [hbm] * 8,
         out_specs=hbm,
         scratch_shapes=[
+            pltpu.VMEM((ROWS, SUB, 128), F32),
             pltpu.VMEM((4, 2 * PC, PC), BF16), pltpu.VMEM((4, 2 * PC, PC), BF16),
             pltpu.VMEM((4, PC, 2 * PC), BF16), pltpu.VMEM((4, PC, 2 * PC), BF16),
             pltpu.VMEM((2, PC, PC), BF16), pltpu.VMEM((2, PC, PC), BF16),
@@ -771,7 +776,7 @@
         ),
         name="polar_filter",
     )(
-        winds.transpose(0, 2, 1, 3), theta.transpose(1, 0, 2), thick.transpose(1, 0, 2), lim,
+        winds.transpose(0, 2, 1, 3), theta.transpose(1, 0, 2), thick.transpose(1, 0, 2), limit,
         jnp.asarray(wv)[:, None, :], jnp.asarray(wp), thi, tlo, uhi, ulo, fhi, flo, ghi, glo,
     )
     new_winds, new_t, new_h = pl.pallas_call(

time: 123 us -> 123 us (level)
  the two profiles are of different devices: /device:TPU:89 before, /device:TPU:67 now
where the time goes in v7:
time: 123 us; the launch traced here: 122 us
  Pallas kernels  120 us (98%)
  other arithmetic  1.43 us (1%)
    pallas_call x1, Pallas kernels, body(): pl.pallas_call(filter_kernel, out_shape=jax.ShapeDtypeStruct((4, ROWS + 2...  109 us
    pallas_call x1, Pallas kernels, body(): pl.pallas_call(stencil_kernel, grid=(ROWS // BLOCK,), out_shape=(jax.Shap...  10.9 us

profile of v7, /device:TPU:67, one launch (start us, length us, event | category | flops | bytes accessed | tf_op | source)
XLA Modules:
  0.0 121.8 jit_solution(17573951498603396051)
XLA Ops:
  0.7 0.9 select_reduce_fusion
  1.6 0.5 convert_element_type.3.cut_ref
  2.1 108.9 %polar_filter.1.state_ref = f32[4,92,16,384]{3,2,1,0:T(8,128)} custom-call(f32[2,90,16,360]{3,2,1,0:T(8,128)} %bitcast.6, f32[90,16,360]{2,1,0:T(8,128)} %bitcast.7, f32[90,16,360]{2,1,0:T(8,128)} %bitcast.8, f32[90]{0:T(128)} %convert_element_type.3.cut_ref, f32[4,1,384]{2,1,0:T(1,128)} %constant.56.wv_ref, f32[2,384]{1,0:T(2,128)} %constant.43.clone.wp_ref, ...), custom_call_target="tpu_custom_call" | custom-call | tf_op jit(solution)/shard_map/polar_filter/pallas_call | solution.py:743
  111.0 10.9 %stencil.1 = (f32[2,90,16,360]{3,2,1,0:T(8,128)}, f32[90,16,360]{2,1,0:T(8,128)}, f32[90,16,360]{2,1,0:T(8,128)}) custom-call(f32[3,1442]{1,0:T(4,128)} %constant.52.clone.trig_ref, f32[4,92,16,384]{3,2,1,0:T(8,128)} %polar_filter.1.state_ref), custom_call_target="tpu_custom_call" | custom-call | tf_op jit(solution)/shard_map/stencil/pallas_call | solution.py:782
  (1 shorter events, 0.0 us)
